TPU v7x, 128 devices: a whole 4x4x4 slice. The times are simulated.
128 devices in a mesh: in: 4 (over z_hi, core), out: 4 (over x), tok: 8 (over y, z_lo).
Axes of the slice: x: 4, y: 4, z: 4 (z_hi: 2, z_lo: 2; z = z_hi * 2 + z_lo), core: 2. Of those that a mesh axis runs over, the one named last changes fastest.
Arguments:
- inputs: bfloat16 [2048, 12288], P('tok', 'in'), may hold values from -6 to 6
- out_grad: bfloat16 [2048, 12288], P('tok', 'in'), may hold values from -2 to 2
- w_gate: bfloat16 [12288, 4096], P('in', ('out', 'tok')), may hold values from -0.0546875 to 0.0546875
- w_up: bfloat16 [12288, 4096], P('in', ('out', 'tok')), may hold values from -0.0546875 to 0.0546875
- w_down: bfloat16 [4096, 12288], P('out', ('in', 'tok')), may hold values from -0.09375 to 0.09375
Outputs:
- d_inputs: bfloat16 [2048, 12288], P('tok', ('in', 'out'))
- grad_gate: bfloat16 [12288, 4096], P('in', ('out', 'tok'))
- grad_up: bfloat16 [12288, 4096], P('in', ('out', 'tok'))
- grad_down: bfloat16 [4096, 12288], P('out', ('in', 'tok'))
All inputs are finite; a program needn't handle non-finite values.
Results may differ from a plain program's by a relative error of at most 0.0049.
Values may be sent and summed in bfloat16 or wider, within the bound.
A program may use at most 128 MiB of HBM per device.

v0:
```python
import jax
import jax.numpy as jnp
from jax import lax
from jax.sharding import PartitionSpec as P


def swiglu_back(gate, up, back):
    sig = jax.nn.sigmoid(gate)
    act = gate * sig
    hidden = (act * up).astype(jnp.bfloat16)
    d_gate = (back * up * sig * (1.0 + gate * (1.0 - sig))).astype(jnp.bfloat16)
    d_up = (back * act).astype(jnp.bfloat16)
    return (hidden, d_gate, d_up)


def shards(inputs, out_grad, w_gate, w_up, w_down):
    contract_rows = (((0,), (0,)), ((), ()))
    gate_full, up_full, down_full = (
        lax.all_gather(w_gate, "tok", axis=1, tiled=True),
        lax.all_gather(w_up, "tok", axis=1, tiled=True),
        lax.all_gather(w_down, "tok", axis=1, tiled=True),
    )
    contract_last = (((1,), (1,)), ((), ()))
    gate_part = jnp.dot(inputs, gate_full, preferred_element_type=jnp.float32)
    up_part = jnp.dot(inputs, up_full, preferred_element_type=jnp.float32)
    back_part = lax.dot_general(
        out_grad, down_full, contract_last, preferred_element_type=jnp.float32
    )
    gate, up, back = lax.psum((gate_part, up_part, back_part), "in")
    hidden, d_gate, d_up = swiglu_back(gate, up, back)
    dx_part = lax.dot_general(d_gate, gate_full, contract_last, preferred_element_type=jnp.float32)
    dx_part = dx_part + lax.dot_general(
        d_up, up_full, contract_last, preferred_element_type=jnp.float32
    )
    d_inputs = lax.psum_scatter(dx_part, "out", scatter_dimension=1, tiled=True).astype(
        jnp.bfloat16
    )
    term_gate = lax.dot_general(inputs, d_gate, contract_rows, preferred_element_type=jnp.float32)
    term_up = lax.dot_general(inputs, d_up, contract_rows, preferred_element_type=jnp.float32)
    term_down = lax.dot_general(hidden, out_grad, contract_rows, preferred_element_type=jnp.float32)
    grad_gate, grad_up, grad_down = (
        lax.psum_scatter(term_gate, "tok", scatter_dimension=1, tiled=True),
        lax.psum_scatter(term_up, "tok", scatter_dimension=1, tiled=True),
        lax.psum_scatter(term_down, "tok", scatter_dimension=1, tiled=True),
    )
    return (
        d_inputs,
        grad_gate.astype(jnp.bfloat16),
        grad_up.astype(jnp.bfloat16),
        grad_down.astype(jnp.bfloat16),
    )


def solution(mesh):
    in_specs = (
        P("tok", "in"),
        P("tok", "in"),
        P("in", ("out", "tok")),
        P("in", ("out", "tok")),
        P("out", ("in", "tok")),
    )
    out_specs = (
        P("tok", ("in", "out")),
        P("in", ("out", "tok")),
        P("in", ("out", "tok")),
        P("out", ("in", "tok")),
    )
    return jax.shard_map(shards, mesh=mesh, in_specs=in_specs, out_specs=out_specs, check_vma=False)
```

profile of v0, /device:TPU:1, one launch (start us, length us, event | category | flops | bytes accessed | tf_op | source)
XLA Modules:
  0.0 1309.9 jit_solution(5944551999970844459)
XLA Ops:
  7.2 0.0 copy-start
  7.2 0.0 all-gather.8.cloned.1.call-start
  7.2 0.7 all-gather.8.cloned.1.call-update
  7.9 0.0 all-gather.6.cloned.1.call-start
  8.0 0.7 all-gather.6.cloned.1.call-update
  8.7 0.0 all-gather.4.cloned.1.call-start
  8.7 0.7 all-gather.4.cloned.1.call-update
  9.4 0.0 all-reduce.3.cloned.1.call-start
  9.4 132.4 %all-gather.8.cloned.1.call-done = bf16[3072,1024]{1,0:T(8,128)(2,1)} async-done(((bf16[3072,128]{1,0:T(8,128)(2,1)}), bf16[3072,1024]{1,0:T(8,128)(2,1)}) %all-gather.8.cloned.1.call-update) | async-done | bytes 6291472 | tf_op jit(solution)/shard_map/all_gather | solution.py:19
  141.9 0.0 copy-done
  141.9 5.5 fusion.6
  147.4 0.0 copy-start.2
  147.4 127.7 %all-gather.6.cloned.1.call-done = bf16[3072,1024]{1,0:T(8,128)(2,1)} async-done(((bf16[3072,128]{1,0:T(8,128)(2,1)}), bf16[3072,1024]{1,0:T(8,128)(2,1)}) %all-gather.6.cloned.1.call-update) | async-done | bytes 6291472 | tf_op jit(solution)/shard_map/all_gather | solution.py:20
  275.1 5.5 fusion.5
  280.7 127.9 %all-gather.4.cloned.1.call-done = bf16[1024,3072]{1,0:T(8,128)(2,1)} async-done(((bf16[1024,384]{1,0:T(8,128)(2,1)}), bf16[1024,3072]{1,0:T(8,128)(2,1)}) %all-gather.4.cloned.1.call-update) | async-done | bytes 6291472 | tf_op jit(solution)/shard_map/all_gather | solution.py:21
  408.5 0.0 copy-done.2
  408.5 5.6 fusion.4
  414.1 0.0 all-reduce.3.cloned.1.call-update
  414.2 0.0 reduce-scatter.5.cloned.1.call-start
  414.2 84.9 %all-reduce.3.cloned.1.call-done = (f32[256,1024]{1,0:T(8,128)}, f32[256,1024]{1,0:T(8,128)}, f32[256,1024]{1,0:T(8,128)}) async-done(((f32[256,1024]{1,0:T(8,128)}, f32[256,1024]{1,0:T(8,128)}, f32[256,1024]{1,0:T(8,128)}), (f32[256,1024]{1,0:T(8,128)}, f32[256,1024]{1,0:T(8,128)}, f32[256,1024]{1,0:T(8,128)})) %all-reduce.3.cloned.1.call-update) | async-done | bytes 3145744 | tf_op jit(solution)/shard_map/psum | solution.py:29
  499.2 0.0 slice-start
  499.2 2.7 multiply_convert_fusion.1
  501.8 0.0 slice-start.1
  501.8 4.8 fusion.7
  506.6 0.0 slice-done
  506.6 0.0 slice-done.1
  506.6 3.5 convolution_add_fusion
  510.1 0.0 reduce-scatter.5.cloned.1.call-update
  510.1 0.0 reduce-scatter.7.cloned.1.call-start
  510.2 6.4 convolution_bitcast_fusion.1
  516.5 0.0 reduce-scatter.7.cloned.1.call-update
  516.6 0.2 reduce-scatter.9.cloned.1.call-start
  516.8 6.3 convolution_bitcast_fusion
  523.1 0.0 copy-start.1
  523.1 0.0 reduce-scatter.9.cloned.1.call-update
  523.1 0.0 reduce-scatter.11.cloned.1.call-start
  523.2 1.2 copy-done.1
  524.3 8.2 fusion.1
  532.6 0.0 reduce-scatter.11.cloned.1.call-update
  532.6 14.8 %reduce-scatter.5.cloned.1.call-done = f32[256,768]{1,0:T(8,128)} async-done(((f32[256,3072]{1,0:T(8,128)}), f32[256,768]{1,0:T(8,128)}) %reduce-scatter.5.cloned.1.call-update) | async-done | bytes 786448 | tf_op jit(solution)/shard_map/reduce_scatter | solution.py:35
  547.4 1.9 convert_element_type.23
  549.3 248.3 %reduce-scatter.7.cloned.1.call-done = f32[3072,128]{0,1:T(8,128)} async-done(((f32[3072,1024]{0,1:T(8,128)}), f32[3072,128]{0,1:T(8,128)}) %reduce-scatter.7.cloned.1.call-update) | async-done | bytes 1572880 | tf_op jit(solution)/shard_map/reduce_scatter | solution.py:42
  797.6 1.5 convert_element_type.24
  799.1 1.2 copy.9
  800.3 248.9 %reduce-scatter.9.cloned.1.call-done = f32[3072,128]{0,1:T(8,128)} async-done(((f32[3072,1024]{0,1:T(8,128)}), f32[3072,128]{0,1:T(8,128)}) %reduce-scatter.9.cloned.1.call-update) | async-done | bytes 1572880 | tf_op jit(solution)/shard_map/reduce_scatter | solution.py:43
  1049.1 1.5 convert_element_type.25
  1050.6 1.2 copy.10
  1051.8 248.9 %reduce-scatter.11.cloned.1.call-done = f32[1024,384]{1,0:T(8,128)} async-done(((f32[1024,3072]{1,0:T(8,128)}), f32[1024,384]{1,0:T(8,128)}) %reduce-scatter.11.cloned.1.call-update) | async-done | bytes 1572880 | tf_op jit(solution)/shard_map/reduce_scatter | solution.py:44
  1300.7 2.4 convert_element_type.27
  (1 shorter events, 0.0 us)
Async XLA Ops:
  7.2 134.7 %copy-start = (bf16[256,3072]{1,0:T(8,128)(2,1)S(1)}, bf16[256,3072]{1,0:T(8,128)(2,1)}, u32[]{:S(2)}) copy-start(bf16[256,3072]{1,0:T(8,128)(2,1)} %param.5) | copy-start | bytes 4718596
  7.2 134.7 %all-gather.8.cloned.1.call-start = ((), (), s32[]{:S(2)}) async-start(), calls=%async_computation.6 | async-start | bytes 7077888 | tf_op jit(solution)/shard_map/all_gather | solution.py:19
  7.9 267.2 %all-gather.6.cloned.1.call-start = ((), (), s32[]{:S(2)}) async-start(), calls=%async_computation.5 | async-start | bytes 7077888 | tf_op jit(solution)/shard_map/all_gather | solution.py:20
  8.7 399.9 %all-gather.4.cloned.1.call-start = ((), (), s32[]{:S(2)}) async-start(), calls=%async_computation.4 | async-start | bytes 7077888 | tf_op jit(solution)/shard_map/all_gather | solution.py:21
  9.4 489.8 %all-reduce.3.cloned.1.call-start = ((), (), s32[]{:S(2)}) async-start(), calls=%async_computation.11 | async-start | bytes 6291456 | tf_op jit(solution)/shard_map/psum | solution.py:29
  147.4 261.1 %copy-start.2 = (bf16[256,3072]{1,0:T(8,128)(2,1)S(1)}, bf16[256,3072]{1,0:T(8,128)(2,1)}, u32[]{:S(2)}) copy-start(bf16[256,3072]{1,0:T(8,128)(2,1)} %param.6) | copy-start | bytes 4718596
  414.2 133.2 %reduce-scatter.5.cloned.1.call-start = ((), (), s32[]{:S(2)}) async-start(), calls=%async_computation.7 | async-start | bytes 3932160 | tf_op jit(solution)/shard_map/reduce_scatter | solution.py:35
  499.2 7.4 slice-start
  501.8 4.8 slice-start.1
  510.1 287.5 %reduce-scatter.7.cloned.1.call-start = ((), (), s32[]{:S(2)}) async-start(), calls=%async_computation.8 | async-start | bytes 14155776 | tf_op jit(solution)/shard_map/reduce_scatter | solution.py:42
  516.6 532.6 %reduce-scatter.9.cloned.1.call-start = ((), (), s32[]{:S(2)}) async-start(), calls=%async_computation.9 | async-start | bytes 14155776 | tf_op jit(solution)/shard_map/reduce_scatter | solution.py:43
  523.1 1.2 copy-start.1
  523.1 777.5 %reduce-scatter.11.cloned.1.call-start = ((), (), s32[]{:S(2)}) async-start(), calls=%async_computation.10 | async-start | bytes 14155776 | tf_op jit(solution)/shard_map/reduce_scatter | solution.py:44
Sparse Core Ops, SparseCore 0:
  9.6 132.2 all-gather.7
  143.4 131.6 all-gather.5
  276.8 131.7 all-gather.3
  414.3 84.8 all-reduce.2
  510.2 37.1 reduce-scatter.4
  549.7 247.8 reduce-scatter.6
  800.0 249.0 reduce-scatter.8
  1051.5 249.0 reduce-scatter.10
where the time goes:
time: 1310 us
  waiting for transfers between devices  1240 us (95%)
  matrix products  45.8 us (3%)
  between operations  14.2 us (1%)
    reduce_scatter x1, waiting for transfers between devices, shards(): lax.psum_scatter(term_down, 'tok', scatter_dimension=1, tiled=True)  249 us
    reduce_scatter x1, waiting for transfers between devices, shards(): lax.psum_scatter(term_up, 'tok', scatter_dimension=1, tiled=True)  249 us
    reduce_scatter x1, waiting for transfers between devices, shards(): lax.psum_scatter(term_gate, 'tok', scatter_dimension=1, tiled=True)  248 us
    all_gather x1, waiting for transfers between devices, shards(): lax.all_gather(w_gate, 'tok', axis=1, tiled=True)  132 us
    all_gather x1, waiting for transfers between devices, shards(): lax.all_gather(w_down, 'tok', axis=1, tiled=True)  128 us
    all_gather x1, waiting for transfers between devices, shards(): lax.all_gather(w_up, 'tok', axis=1, tiled=True)  128 us
    psum x1, waiting for transfers between devices, shards(): gate, up, back = lax.psum((gate_part, up_part, back_part), 'in')  84.9 us
  transfers between devices with their start and end apart: 8, of which 8 were waited for; matrix products, arithmetic and copies ran while one was open for 3% of the time, Pallas kernels for 0%

commit v1 on v0

v1 whole, which is shorter than its diff:
```python
import jax
import jax.numpy as jnp
from jax import lax
from jax.experimental import pallas as pl
from jax.experimental.pallas import tpu as pltpu
from jax.sharding import PartitionSpec as P

MESH = pl.DeviceIdType.MESH
F32 = jnp.float32
BF16 = jnp.bfloat16
N_SEM = 168
ORDER = (0, 1, 3, 2)


def kernel(
    inputs, out_grad, w_gate, w_up, w_down,
    d_in, g_gate, g_up, g_down,
    xin, wcat, og, wdn, pbuf, pr, s2, xr, yr, zg, zgr, zb, zbr, dcat, hid, dxs, dx0, dxr, dxzr, gs,
    ssem, rsem, lsem,
):
    i = lax.axis_index("in")
    x = lax.axis_index("out")
    t = lax.axis_index("tok")
    h, c, y, l = i // 2, i % 2, t // 2, t % 2
    z = 2 * h + l

    def dev(dx=0, dy=0, dz=0, dc=0):
        zz = (z + dz) % 4
        return (2 * (zz // 2) + (c + dc) % 2, (x + dx) % 4, 2 * ((y + dy) % 4) + zz % 2)

    def lpart():
        return (i, x, 2 * y + 1 - l)

    def al(v, n):
        return pl.multiple_of(v, n)

    index, sent, local = {}, [], []

    def sem_of(key):
        if key not in index:
            index[key] = len(index)
        return index[key]

    def send(key, src, dst, device):
        n = sem_of(key)
        copy = pltpu.make_async_remote_copy(
            src_ref=src, dst_ref=dst, send_sem=ssem.at[n], recv_sem=rsem.at[n],
            device_id=device, device_id_type=MESH,
        )
        copy.start()
        sent.append(copy)
        return copy

    def recv(key, dst):
        n = sem_of(key)
        pltpu.make_async_remote_copy(
            src_ref=dst, dst_ref=dst, send_sem=ssem.at[n], recv_sem=rsem.at[n],
            device_id=dev(dc=1), device_id_type=MESH,
        ).wait_recv()

    def move(src, dst):
        copy = pltpu.make_async_copy(src, dst, lsem.at[len(local)])
        copy.start()
        local.append(copy)
        return copy

    own_in = move(inputs.at[:, pl.ds(al(x * 768, 128), 768)], xin.at[pl.ds(al(l * 256, 256), 256), :])
    own_og = move(out_grad.at[:, pl.ds(al(t * 384, 128), 384)], og.at[pl.ds(al(l * 256, 256), 256), :])
    own_dn = move(w_down, wdn)
    own_w = [
        move(w.at[pl.ds(al(x * 768, 256), 768), :], wcat.at[:, pl.ds(128 * q, 128)])
        for q, w in enumerate((w_gate, w_up))
    ]

    barrier = pltpu.get_barrier_semaphore()
    peers = [dev(dc=1)]
    peers += [dev(dx=m) for m in (1, 2, 3)]
    peers += [dev(dy=m) for m in (1, 2, 3)]
    peers += [dev(dz=m) for m in (1, 2, 3)]
    cross = [(i, x, 2 * ((y + m) % 4) + 1 - l) for m in (1, 2, 3)]
    peers += cross
    for peer in peers:
        pl.semaphore_signal(barrier, inc=1, device_id=peer, device_id_type=MESH)
    pl.semaphore_wait(barrier, len(peers))

    def own_rows(m, part):
        return pl.ds(al(((4 - m) % 4) * 512 + part * 256, 256), 256)

    send(("og", 0, 1), out_grad.at[:, pl.ds(al((2 * y + 1 - l) * 384, 128), 384)], og.at[own_rows(0, l), :], lpart())
    send(
        ("in", 0, 1), inputs.at[:, pl.ds(al(x * 768, 128), 768)],
        xin.at[own_rows(0, l), :], lpart(),
    )
    for m in (2, 1, 3):
        there = (y + m) % 4
        send(("og", m, 0), out_grad.at[:, pl.ds(al((2 * there + l) * 384, 128), 384)], og.at[own_rows(m, l), :], dev(dy=m))
        send(("og", m, 1), out_grad.at[:, pl.ds(al((2 * there + 1 - l) * 384, 128), 384)], og.at[own_rows(m, l), :], cross[m - 1])
    for j in (2, 1, 3):
        for q, w in enumerate((w_gate, w_up)):
            send(
                ("w", j, q), w.at[pl.ds(al(((x + j) % 4) * 768, 256), 768), :],
                wcat.at[:, pl.ds(256 * (4 - j) + 128 * q, 128)], dev(dx=j),
            )
    own_in.wait()
    for m in (1, 3, 2):
        send(("in", m, 0), xin.at[pl.ds(al(l * 256, 256), 256), :], xin.at[own_rows(m, l), :], dev(dy=m))
    recv(("in", 0, 1), xin.at[pl.ds(al((1 - l) * 256, 256), 256), :])
    for m in (1, 3, 2):
        send(("in", m, 1), xin.at[pl.ds(al((1 - l) * 256, 256), 256), :], xin.at[own_rows(m, 1 - l), :], dev(dy=m))

    for copy in [own_og, own_dn] + own_w:
        copy.wait()

    def rows(k, part=0):
        return pl.ds(al(k * 512 + part * 256, 256), 256)

    uses = []

    def partial_slot():
        n = len(uses)
        if n >= 2:
            uses[n - 2].wait_send()
        return n % 2

    def core_reduce_start(key, slot, n):
        uses.append(send((key, n), pbuf.at[slot, pl.ds(al((1 - c) * 256, 256), 256), :], pr.at[n], dev(dc=1)))

    slots = {}

    def b1(k):
        if k:
            recv(("og", 4 - k, 0), og.at[rows(k, l), :])
            recv(("og", 4 - k, 1), og.at[rows(k, 1 - l), :])
        else:
            recv(("og", 0, 1), og.at[rows(0, 1 - l), :])
        slot = partial_slot()
        slots["b", k] = slot

        @pl.loop(0, 4)
        def _(m):
            there = (y + m) % 4
            pbuf[slot, :, pl.ds(al(m * 256, 256), 256)] = lax.dot_general(
                og[pl.ds(512 * k, 512), :], wdn[pl.ds(al(there * 256, 256), 256), :],
                (((1,), (1,)), ((), ())), preferred_element_type=F32,
            )

        core_reduce_start("cr", slot, 4 + k)

    def core_sum(slot, n):
        recv(("cr", n), pr.at[n])

        @pl.loop(0, 8)
        def _(r):
            at = pl.ds(al(r * 32, 32), 32)
            mine = pl.ds(al(c * 256 + r * 32, 32), 32)
            total = pbuf[slot, mine, :] + pr[n, at, :]
            pr[n, at, :] = total
            s2[n, at, :] = total.astype(BF16)

    def b2(k):
        core_sum(slots["b", k], 4 + k)
        for m in (2, 1, 3):
            send(("yr", (k - m) % 4, m), s2.at[4 + k, :, pl.ds(256 * m, 256)], yr.at[(k - m) % 4, m - 1], dev(dy=m))

    def g1(k):
        if k:
            recv(("in", 4 - k, 0), xin.at[rows(k, l), :])
            recv(("in", 4 - k, 1), xin.at[rows(k, 1 - l), :])
        slot = partial_slot()
        slots["g", k] = slot

        @pl.loop(0, 4)
        def _(n):
            at = pl.ds(al(n * 256, 256), 256)
            pbuf[slot, :, at] = jnp.dot(xin[pl.ds(512 * k, 512), :], wcat[:, at], preferred_element_type=F32)

        core_reduce_start("cr", slot, k)

    def g2(k):
        core_sum(slots["g", k], k)
        for j in (2, 1, 3):
            send(("xr", k, j), s2.at[k, :, pl.ds(256 * j, 256)], xr.at[k, j - 1], dev(dx=j))

    def b3(k):
        for m in (1, 2, 3):
            recv(("yr", k, m), yr.at[k, m - 1])
        zb[k] = (pr[4 + k, :, 0:256] + yr[k, 0].astype(F32)) + (yr[k, 1].astype(F32) + yr[k, 2].astype(F32))
        for d in (2, 1, 3):
            zz = (z + d) % 4
            send(
                ("zb", k, d), zb.at[k, pl.ds(al((zz // 2) * 128, 128), 128), pl.ds(al((zz % 2) * 128, 128), 128)],
                zbr.at[k, d - 1], dev(dz=d),
            )

    def g3(k):
        for j in (1, 2, 3):
            recv(("xr", k, j), xr.at[k, j - 1])
        zg[k] = (pr[k, :, 0:256] + xr[k, 0].astype(F32)) + (xr[k, 1].astype(F32) + xr[k, 2].astype(F32))
        send(("zg", k), zg.at[k, pl.ds(al((1 - h) * 128, 128), 128), :], zgr.at[k], dev(dz=2))

    def e(k):
        recv(("zg", k), zgr.at[k])
        for d in (1, 2, 3):
            recv(("zb", k, d), zbr.at[k, d - 1])
        mine = pl.ds(al(h * 128, 128), 128)
        both = zg[k, mine, :] + zgr[k]
        gate, up = both[:, :128], both[:, 128:]
        back = (zb[k, mine, pl.ds(al(l * 128, 128), 128)] + zbr[k, 0]) + (zbr[k, 1] + zbr[k, 2])
        sig = jax.nn.sigmoid(gate)
        act = gate * sig
        at = pl.ds(al(k * 512 + c * 256 + h * 128, 128), 128)
        dcat[at, 0:128] = (back * up * sig * (1.0 + gate * (1.0 - sig))).astype(BF16)
        dcat[at, 128:256] = (back * act).astype(BF16)
        cols = pl.ds(al(l * 128, 128), 128)
        hid[at, cols] = (act * up).astype(BF16)
        send(("ag", k), dcat.at[at, 0:256], dcat.at[at, 0:256], dev(dz=2))
        for d in (2, 1, 3):
            send(("ah", k, d), hid.at[at, cols], hid.at[at, cols], dev(dz=d))

    def half(k, part):
        return pl.ds(al(k * 512 + part * 256, 256), 256)

    def a2(k):
        there = pl.ds(al(k * 512 + c * 256 + (1 - h) * 128, 128), 128)
        recv(("ag", k), dcat.at[there, 0:256])
        for j in (2, 1, 3):
            send(("xg", k, j), dcat.at[half(k, c), 0:256], dcat.at[half(k, c), pl.ds(256 * (4 - j), 256)], dev(dx=j))
        for d in (1, 2, 3):
            zz = (z - d + 4) % 4
            at = pl.ds(al(k * 512 + c * 256 + (zz // 2) * 128, 128), 128)
            recv(("ah", k, d), hid.at[at, pl.ds(al((zz % 2) * 128, 128), 128)])
        for m in (2, 1, 3):
            kk = (k - m) % 4
            send(("yg", kk, m), hid.at[half(k, c), 0:256], hid.at[half(kk, c), pl.ds(256 * (4 - m), 256)], dev(dy=m))

    def a3(k):
        for j in (1, 2, 3):
            recv(("xg", k, j), dcat.at[half(k, c), pl.ds(256 * (4 - j), 256)])
        send(("cg", k), dcat.at[half(k, c), :], dcat.at[half(k, c), :], dev(dc=1))

    def xk(k):
        recv(("cg", k), dcat.at[half(k, 1 - c), :])

        @pl.loop(0, 3)
        def _(n):
            at = pl.ds(al(n * 256, 256), 256)
            part = lax.dot_general(
                dcat[pl.ds(512 * k, 512), :], wcat[at, :], (((1,), (1,)), ((), ())), preferred_element_type=F32
            )
            if k:
                dxs[k - 1, :, at] = part.astype(BF16)
            else:
                dx0[:, at] = part

        if k:
            send(("dx", k), dxs.at[k - 1], dxr.at[k - 1], dev(dy=k))

    def a4(k):
        for m in (1, 2, 3):
            recv(("yg", k, m), hid.at[half(k, c), pl.ds(256 * (4 - m), 256)])
        send(("ch", k), hid.at[half(k, c), :], hid.at[half(k, c), :], dev(dc=1))

    o = ORDER
    b1(o[0])
    b1(o[1])
    b2(o[0])
    b1(o[2])
    b2(o[1])
    b1(o[3])
    b2(o[2])
    for j in (1, 2, 3):
        for q in (0, 1):
            recv(("w", j, q), wcat.at[:, pl.ds(256 * (4 - j) + 128 * q, 128)])

    def g3b3(k):
        g3(k)
        b3(k)

    stages = (g1, g2, g3b3, e, a2, a3, xk)
    for step in range(len(stages) + 3):
        for s in reversed(range(len(stages))):
            if 0 <= step - s < 4:
                stages[s](o[step - s])
        if step == 0:
            b2(o[3])

    def grad_slot(j):
        @pl.loop(0, 3)
        def _(n):
            at = pl.ds(al(n * 256, 256), 256)
            gs[j, at, :] = lax.dot_general(
                xin[:, at], dcat[:, 256 * j : 256 * j + 256], (((0,), (0,)), ((), ())), preferred_element_type=F32
            ).astype(BF16)

        here = pl.ds(al(x * 768, 256), 768)
        for q, out in enumerate((g_gate, g_up)):
            src = gs.at[j, :, pl.ds(128 * q, 128)]
            if j:
                send(("gw", j, q), src, out.at[here, :], dev(dx=j))
            else:
                move(src, out.at[here, :])

    for j in (2, 1, 3, 0):
        grad_slot(j)

    for k in o:
        a4(k)
    for k in range(4):
        recv(("ch", k), hid.at[half(k, 1 - c), :])

    @pl.loop(0, 4)
    def _(m):
        there = (y + m) % 4
        g_down[pl.ds(al(there * 256, 256), 256), :] = lax.dot_general(
            hid[:, pl.ds(al(m * 256, 256), 256)], og[...], (((0,), (0,)), ((), ())), preferred_element_type=F32
        ).astype(BF16)

    for k in (1, 2, 3):
        recv(("dx", k), dxr.at[k - 1])

    @pl.loop(0, 16)
    def _(r):
        at = pl.ds(al(r * 32, 32), 32)
        dx0[at, :] = (dx0[at, :] + dxr[0, at, :].astype(F32)) + (dxr[1, at, :].astype(F32) + dxr[2, at, :].astype(F32))

    send(("dz",), dx0.at[pl.ds(al((1 - l) * 256, 256), 256), :], dxzr, lpart())
    recv(("dz",), dxzr)

    @pl.loop(0, 8)
    def _(r):
        at = pl.ds(al(r * 32, 32), 32)
        d_in[at, :] = (dx0[pl.ds(al(l * 256 + r * 32, 32), 32), :] + dxzr[at, :]).astype(BF16)

    for j in (1, 2, 3):
        for q, out in enumerate((g_gate, g_up)):
            recv(("gw", j, q), out.at[pl.ds(al(((x - j + 4) % 4) * 768, 256), 768), :])
    for copy in local[5:]:
        copy.wait()
    done = [id(copy) for copy in uses[:-2]]
    for copy in sent:
        if id(copy) not in done:
            copy.wait_send()
    assert len(index) <= N_SEM, len(index)


def shards(inputs, out_grad, w_gate, w_up, w_down):
    v = pltpu.VMEM
    any_ = pl.BlockSpec(memory_space=pl.ANY)
    vm = pl.BlockSpec(memory_space=pltpu.VMEM)
    return pl.pallas_call(
        kernel,
        name="swiglu_back",
        out_shape=(
            jax.ShapeDtypeStruct((256, 768), BF16),
            jax.ShapeDtypeStruct((3072, 128), BF16),
            jax.ShapeDtypeStruct((3072, 128), BF16),
            jax.ShapeDtypeStruct((1024, 384), BF16),
        ),
        in_specs=[any_] * 5,
        out_specs=(vm, any_, any_, vm),
        scratch_shapes=[
            v((2048, 768), BF16),
            v((768, 1024), BF16),
            v((2048, 384), BF16),
            v((1024, 384), BF16),
            v((2, 512, 1024), F32),
            v((8, 256, 1024), F32),
            v((8, 256, 1024), BF16),
            v((4, 3, 256, 256), BF16),
            v((4, 3, 256, 256), BF16),
            v((4, 256, 256), F32),
            v((4, 128, 256), F32),
            v((4, 256, 256), F32),
            v((4, 3, 128, 128), F32),
            v((2048, 1024), BF16),
            v((2048, 1024), BF16),
            v((3, 512, 768), BF16),
            v((512, 768), F32),
            v((3, 512, 768), BF16),
            v((256, 768), F32),
            v((4, 768, 256), BF16),
            pltpu.SemaphoreType.DMA((N_SEM,)),
            pltpu.SemaphoreType.DMA((N_SEM,)),
            pltpu.SemaphoreType.DMA((8,)),
        ],
        compiler_params=pltpu.CompilerParams(collective_id=0, has_side_effects=True, vmem_limit_bytes=60 * 2**20),
        cost_estimate=pl.CostEstimate(flops=13 * 10**9, bytes_accessed=8 * 2**20, transcendentals=65536),
    )(inputs, out_grad, w_gate, w_up, w_down)


def solution(mesh):
    in_specs = (
        P("tok", "in"),
        P("tok", "in"),
        P("in", ("out", "tok")),
        P("in", ("out", "tok")),
        P("out", ("in", "tok")),
    )
    out_specs = (
        P("tok", ("in", "out")),
        P("in", ("out", "tok")),
        P("in", ("out", "tok")),
        P("out", ("in", "tok")),
    )
    return jax.shard_map(shards, mesh=mesh, in_specs=in_specs, out_specs=out_specs, check_vma=False)
```

time: 1310 us -> 195 us (0.15)
  waiting for transfers between devices: 1240 us -> 0 us
  Pallas kernels: 0 us -> 186 us
  matrix products: 45.8 us -> 0 us
  between operations: 14.2 us -> 0.65 us
    reduce_scatter x4 -> x0, waiting for transfers between devices: 761 us -> none  [the longest x1 249 us: shards(): lax.psum_scatter(term_down, 'tok', scatter_dimension=1, tiled=True)]
    all_gather x3 -> x0, waiting for transfers between devices: 388 us -> none  [the longest x1 132 us: shards(): lax.all_gather(w_gate, 'tok', axis=1, tiled=True)]
    pallas_call x0 -> x1, Pallas kernels: none -> 186 us  [shards(): pl.pallas_call(kernel, name='swiglu_back', out_shape=(jax.ShapeDtypeStruc...]
    psum x1 -> x0, waiting for transfers between devices: 84.9 us -> none  [shards(): gate, up, back = lax.psum((gate_part, up_part, back_part), 'in')]
    dot_general x8 -> x0, matrix products: 45.8 us -> none  [the longest x1 8.22 us: shards(): lax.dot_general(hidden, out_grad, contract_rows, preferred_element_type=j...]
  transfers between devices with their start and end apart: 8 -> 0, of which waited for: 8 -> 0; matrix products, arithmetic and copies ran while one was open for 3% -> 0% of each run, Pallas kernels for 0% -> 0%
where the time goes in v1:
time: 195 us; the launch traced here: 192 us
  Pallas kernels  186 us (95%)
  local copies, waits for them, and re-layouts  5.74 us (3%)
    pallas_call x1, Pallas kernels, shards(): pl.pallas_call(kernel, name='swiglu_back', out_shape=(jax.ShapeDtypeStruc...  186 us
    unnamed x8, local copies, waits for them, and re-layouts  5.74 us

profile of v1, /device:TPU:1, one launch (start us, length us, event | category | flops | bytes accessed | tf_op | source)
XLA Modules:
  0.0 192.5 jit_solution(2692459777750493499)
XLA Ops:
  0.6 186.1 %swiglu_back.1 = (bf16[256,768]{1,0:T(8,128)(2,1)}, bf16[3072,128]{1,0:T(8,128)(2,1)}, bf16[3072,128]{1,0:T(8,128)(2,1)}, bf16[1024,384]{1,0:T(8,128)(2,1)}) custom-call(bf16[256,3072]{1,0:T(8,128)(2,1)} %inputs.1, bf16[256,3072]{1,0:T(8,128)(2,1)} %out_grad.1, bf16[3072,128]{1,0:T(8,128)(2,1)} %w_gate.1, bf16[3072,128]{1,0:T(8,128)(2,1)} %w_up.1, ...), custom_call_target="tpu_custom_call" | custom-call | flops 12999999488 | bytes 8388608 | tf_op jit(solution)/shard_map/swiglu_back/pallas_call | solution.py:350
  186.7 0.0 copy-start.1
  186.7 1.8 copy.13
  188.6 0.0 copy-start
  188.6 2.1 %copy.14 = bf16[3072,128]{1,0:T(8,128)(2,1)} copy(bf16[3072,128]{1,0:T(8,128)(2,1)} %get-tuple-element.9) | data formatting | bytes 1572864
  190.7 0.0 copy-done.1
  190.7 0.9 copy.15
  191.6 0.0 copy-done
  191.6 0.9 copy.16
Async XLA Ops:
  186.7 4.0 %copy-start.1 = (bf16[3072,128]{1,0:T(8,128)(2,1)S(1)}, bf16[3072,128]{1,0:T(8,128)(2,1)}, u32[]{:S(2)}) copy-start(bf16[3072,128]{1,0:T(8,128)(2,1)} %get-tuple-element.10) | copy-start | bytes 2359300
  188.6 3.0 %copy-start = (bf16[1024,384]{1,0:T(8,128)(2,1)S(1)}, bf16[1024,384]{1,0:T(8,128)(2,1)}, u32[]{:S(2)}) copy-start(bf16[1024,384]{1,0:T(8,128)(2,1)} %get-tuple-element.11) | copy-start | bytes 2359300

commit v2 on v1

v2 whole, which is shorter than its diff:
```python
import jax
import jax.numpy as jnp
from jax import lax
from jax.experimental import pallas as pl
from jax.experimental.pallas import tpu as pltpu
from jax.sharding import PartitionSpec as P

MESH = pl.DeviceIdType.MESH
F32 = jnp.float32
BF16 = jnp.bfloat16
N_SEM = 230
N_SLOT = 3
DZ = (0, 2)
DY = tuple(k for k in range(4) if k not in DZ)
Z_FIRST = (0, 1, 2, 3)
FWD_IN, FWD_XG, FWD_YG, FWD_OG = True, False, True, False


def kernel(
    inputs, out_grad, w_gate, w_up, w_down,
    d_in, g_gate, g_up, g_down,
    xin, wcat, og, wdn, pbuf, pr, s2, xr, yr, zg, zgr, zb, zbr, dcat, hid, dzs, dzr, dxo, dxf, dxs, dxr, gs, gacc,
    ssem, rsem, lsem,
):
    i = lax.axis_index("in")
    x = lax.axis_index("out")
    t = lax.axis_index("tok")
    h, c, y, l = i // 2, i % 2, t // 2, t % 2
    z = 2 * h + l

    def dev(dx=0, dy=0, dz=0, dc=0):
        zz = (z + dz) % 4
        return (2 * (zz // 2) + (c + dc) % 2, (x + dx) % 4, 2 * ((y + dy) % 4) + zz % 2)

    def lpart():
        return (i, x, 2 * y + 1 - l)

    def al(v, n):
        return pl.multiple_of(v, n)

    index, sent, local, got = {}, [], [], set()

    def sem_of(key):
        if key not in index:
            index[key] = len(index)
        return index[key]

    def send(key, src, dst, device):
        n = sem_of(key)
        copy = pltpu.make_async_remote_copy(
            src_ref=src, dst_ref=dst, send_sem=ssem.at[n], recv_sem=rsem.at[n],
            device_id=device, device_id_type=MESH,
        )
        copy.start()
        sent.append(copy)
        return copy

    def recv(key, dst):
        if key in got:
            return
        got.add(key)
        n = sem_of(key)
        pltpu.make_async_remote_copy(
            src_ref=dst, dst_ref=dst, send_sem=ssem.at[n], recv_sem=rsem.at[n],
            device_id=dev(dc=1), device_id_type=MESH,
        ).wait_recv()

    def move(src, dst):
        copy = pltpu.make_async_copy(src, dst, lsem.at[len(local)])
        copy.start()
        local.append(copy)
        return copy

    def rows(s, yy, ll):
        return pl.ds(al(s * 512 + ll * 256 + yy * 64, 64), 64)

    def half(s, part):
        return pl.ds(al(s * 512 + part * 256, 256), 256)

    cols_in = pl.ds(al(x * 768, 128), 768)
    mine16 = pl.ds(al(x * 16, 16), 16)
    own_in = []
    for s in range(4):
        here = pl.ds(64 * s, 64)
        own_in.append(move(inputs.at[here, cols_in], xin.at[rows(s, y, l), :]))
    own_og = move(out_grad.at[:, x, :, pl.ds(al(t * 384, 128), 384)], og.at[:, 4 * l + y, mine16, :])
    own_dn = move(w_down, wdn)
    own_w = [
        move(w.at[pl.ds(al(x * 768, 256), 768), :], wcat.at[:, pl.ds(128 * q, 128)])
        for q, w in enumerate((w_gate, w_up))
    ]
    n_first = len(local)

    barrier = pltpu.get_barrier_semaphore()
    peers = [dev(dc=1)]
    peers += [dev(dx=m) for m in (1, 2, 3)]
    peers += [dev(dy=m) for m in (1, 2, 3)]
    peers += [dev(dz=m) for m in (1, 2, 3)]
    cross = [(i, x, 2 * ((y + m) % 4) + 1 - l) for m in (1, 2, 3)]
    peers += cross
    for peer in peers:
        pl.semaphore_signal(barrier, inc=1, device_id=peer, device_id_type=MESH)
    pl.semaphore_wait(barrier, len(peers))

    def og_cols(yy, ll):
        return pl.ds(al((2 * yy + ll) * 384, 128), 384)

    def st_og():
        send(("og", 0, 1), out_grad.at[:, x, :, og_cols(y, 1 - l)], og.at[:, 4 * l + y, mine16, :], lpart())
        for m in (2, 1, 3):
            there = (y + m) % 4
            send(("og", m, 0), out_grad.at[:, x, :, og_cols(there, l)], og.at[:, 4 * l + y, mine16, :], dev(dy=m))
            send(("og", m, 1), out_grad.at[:, x, :, og_cols(there, 1 - l)], og.at[:, 4 * l + y, mine16, :], cross[m - 1])

    def take_og():
        own_og.wait()
        recv(("og", 0, 1), og.at[:, 4 * (1 - l) + y, mine16, :])
        for m in (1, 3, 2):
            yy = (y - m + 4) % 4
            recv(("og", m, 0), og.at[:, 4 * l + yy, mine16, :])
            recv(("og", m, 1), og.at[:, 4 * (1 - l) + yy, mine16, :])

    def og_part(s, j, lo=0, n=16):
        return og.at[s, :, pl.ds(al(((x + j) % 4) * 16 + lo, n), n), :]

    def ox(s):
        if s == 0:
            take_og()
        for j in (1, 3) if FWD_OG else (2, 1, 3):
            send(("ox", s, j), og_part(s, 0), og_part(s, 0), dev(dx=j))

    def fo(s):
        if FWD_OG:
            for j in (1, 3):
                part = og.at[s, pl.ds(0 if j == 1 else 4, 4), pl.ds(al(((x - j + 4) % 4) * 16, 16), 16), :]
                recv(("ox", s, j), og_part(s, 4 - j))
                send(("of", s, j), part, part, dev(dx=j))

    def wait_og(s):
        if FWD_OG:
            for j in (1, 3):
                recv(("of", s, j), og.at[s, pl.ds(0 if j == 1 else 4, 4), pl.ds(al(((x + 2) % 4) * 16, 16), 16), :])
        else:
            for j in (1, 3, 2):
                recv(("ox", s, j), og_part(s, 4 - j))

    def stz(s):
        here = pl.ds(64 * s, 64)
        at = rows(s, y, l)
        send(("in", s, 0, 1), inputs.at[here, cols_in], xin.at[at, :], lpart())

    def sty(s):
        here = pl.ds(64 * s, 64)
        at = rows(s, y, l)
        for m in (1, 3) if FWD_IN else (2, 1, 3):
            send(("in", s, m, 0), inputs.at[here, cols_in], xin.at[at, :], dev(dy=m))

    def st_w(q):
        w = (w_gate, w_up)[q]
        for j in (2, 1, 3):
            send(
                ("w", j, q), w.at[pl.ds(al(((x + j) % 4) * 768, 256), 768), :],
                wcat.at[:, pl.ds(256 * (4 - j) + 128 * q, 128)], dev(dx=j),
            )

    def part_rows(s, yy, ll, m):
        return pl.ds(al(s * 512 + ll * 256 + yy * 64 + (0 if m == 1 else 32), 32), 32)

    def fw(s):
        if s in Z_FIRST:
            at = rows(s, y, 1 - l)
            recv(("in", s, 0, 1), xin.at[at, :])
            for m in (1, 3) if FWD_IN else (2, 1, 3):
                send(("in", s, m, 1), xin.at[at, :], xin.at[at, :], dev(dy=m))

    def fi(s):
        if FWD_IN:
            for q in (0, 1) if s in Z_FIRST else (0,):
                for m in (1, 3):
                    yy, ll = (y - m + 4) % 4, (1 - l if q else l)
                    recv(("in", s, m, q), xin.at[rows(s, yy, ll), :])
                    at = part_rows(s, yy, ll, m)
                    send(("if", s, m, q), xin.at[at, :], xin.at[at, :], dev(dy=m))

    def far_in(s, q):
        yy, ll = (y + 2) % 4, (1 - l if q else l)
        if FWD_IN:
            for m in (1, 3):
                recv(("if", s, m, q), xin.at[part_rows(s, yy, ll, m), :])
        else:
            recv(("in", s, 2, q), xin.at[rows(s, yy, ll), :])

    def fz(s):
        if s not in Z_FIRST:
            for m in (1, 3, 2):
                at = rows(s, (y - m + 4) % 4, l)
                if m == 2:
                    far_in(s, 0)
                elif not FWD_IN:
                    recv(("in", s, m, 0), xin.at[at, :])
                send(("in", s, m, 1), xin.at[at, :], xin.at[at, :], lpart())

    def wait_in(s):
        own_in[s].wait()
        if s in Z_FIRST:
            if not FWD_IN:
                for m in (1, 3):
                    for q in (0, 1):
                        recv(("in", s, m, q), xin.at[rows(s, (y - m + 4) % 4, 1 - l if q else l), :])
            far_in(s, 0)
            far_in(s, 1)
        else:
            recv(("in", s, 0, 1), xin.at[rows(s, y, 1 - l), :])
            for m in (1, 3, 2):
                recv(("in", s, m, 1), xin.at[rows(s, (y - m + 4) % 4, 1 - l), :])

    uses = []

    def partial_slot():
        n = len(uses)
        if n >= N_SLOT:
            uses[n - N_SLOT].wait_send()
        return n % N_SLOT

    def core_send(slot, n):
        uses.append(send(("cr", n), pbuf.at[slot, pl.ds(al((1 - c) * 256, 256), 256), :], pr.at[n], dev(dc=1)))

    slots, seen = {}, []

    def b1(s):
        wait_og(s)
        if s == 0:
            own_dn.wait()
        slot = partial_slot()
        slots["b", s] = slot

        @pl.loop(0, 4)
        def _(m):
            there = (y + m) % 4
            pbuf[slot, :, pl.ds(al(m * 256, 256), 256)] = lax.dot_general(
                og[s].reshape(512, 384), wdn[pl.ds(al(there * 256, 256), 256), :],
                (((1,), (1,)), ((), ())), preferred_element_type=F32,
            )

        core_send(slot, 4 + s)

    def g1(s):
        wait_in(s)
        if s == 0:
            for copy in own_w:
                copy.wait()
            for j in (1, 3, 2):
                for q in (0, 1):
                    recv(("w", j, q), wcat.at[:, pl.ds(256 * (4 - j) + 128 * q, 128)])
        slot = partial_slot()
        slots["g", s] = slot

        @pl.loop(0, 4)
        def _(n):
            at = pl.ds(al(n * 256, 256), 256)
            pbuf[slot, :, at] = jnp.dot(xin[pl.ds(512 * s, 512), :], wcat[:, at], preferred_element_type=F32)

        core_send(slot, s)

    def core_sum(slot, n):
        recv(("cr", n), pr.at[n])

        @pl.loop(0, 8)
        def _(r):
            at = pl.ds(al(r * 32, 32), 32)
            mine = pl.ds(al(c * 256 + r * 32, 32), 32)
            total = pbuf[slot, mine, :] + pr[n, at, :]
            pr[n, at, :] = total
            s2[n, at, :] = total.astype(BF16)

    def b2(s):
        core_sum(slots["b", s], 4 + s)
        for m in (2, 1, 3):
            send(("yr", s, m), s2.at[4 + s, :, pl.ds(256 * m, 256)], yr.at[s, m - 1], dev(dy=m))

    def g2(s):
        core_sum(slots["g", s], s)
        for j in (2, 1, 3):
            send(("xr", s, j), s2.at[s, :, pl.ds(256 * j, 256)], xr.at[s, j - 1], dev(dx=j))

    def b3(k):
        for m in (1, 3, 2):
            recv(("yr", k, m), yr.at[k, m - 1])
        zb[k] = (pr[4 + k, :, 0:256] + yr[k, 0].astype(F32)) + (yr[k, 1].astype(F32) + yr[k, 2].astype(F32))
        for d in (2, 1, 3):
            zz = (z + d) % 4
            send(
                ("zb", k, d), zb.at[k, pl.ds(al((zz // 2) * 128, 128), 128), pl.ds(al((zz % 2) * 128, 128), 128)],
                zbr.at[k, d - 1], dev(dz=d),
            )

    def g3(k):
        for j in (1, 3, 2):
            recv(("xr", k, j), xr.at[k, j - 1])
        zg[k] = (pr[k, :, 0:256] + xr[k, 0].astype(F32)) + (xr[k, 1].astype(F32) + xr[k, 2].astype(F32))
        send(("zg", k), zg.at[k, pl.ds(al((1 - h) * 128, 128), 128), :], zgr.at[k], dev(dz=2))

    def e(k):
        recv(("zg", k), zgr.at[k])
        for d in (1, 2, 3):
            recv(("zb", k, d), zbr.at[k, d - 1])
        mine = pl.ds(al(h * 128, 128), 128)
        both = zg[k, mine, :] + zgr[k]
        gate, up = both[:, :128], both[:, 128:]
        back = (zb[k, mine, pl.ds(al(l * 128, 128), 128)] + zbr[k, 0]) + (zbr[k, 1] + zbr[k, 2])
        sig = jax.nn.sigmoid(gate)
        act = gate * sig
        at = pl.ds(al(k * 512 + c * 256 + h * 128, 128), 128)
        dcat[at, 0:128] = (back * up * sig * (1.0 + gate * (1.0 - sig))).astype(BF16)
        dcat[at, 128:256] = (back * act).astype(BF16)
        cols = pl.ds(al(l * 128, 128), 128)
        hid[at, cols] = (act * up).astype(BF16)
        send(("ag", k), dcat.at[at, 0:256], dcat.at[at, 0:256], dev(dz=2))
        for d in (2, 1, 3):
            send(("ah", k, d), hid.at[at, cols], hid.at[at, cols], dev(dz=d))

    def a2x(k):
        there = pl.ds(al(k * 512 + c * 256 + (1 - h) * 128, 128), 128)
        recv(("ag", k), dcat.at[there, 0:256])
        for j in (1, 3) if FWD_XG else (2, 1, 3):
            send(("xg", k, j), dcat.at[half(k, c), 0:256], dcat.at[half(k, c), pl.ds(256 * (4 - j), 256)], dev(dx=j))

    def a2y(k):
        for d in (1, 2, 3):
            zz = (z - d + 4) % 4
            at = pl.ds(al(k * 512 + c * 256 + (zz // 2) * 128, 128), 128)
            recv(("ah", k, d), hid.at[at, pl.ds(al((zz % 2) * 128, 128), 128)])
        for m in (1, 3) if FWD_YG else (2, 1, 3):
            send(("yg", k, m), hid.at[half(k, c), 0:256], hid.at[half(k, c), pl.ds(256 * (4 - m), 256)], dev(dy=m))

    def fwd_half(k, j):
        return pl.ds(al(k * 512 + c * 256 + (0 if j == 1 else 128), 128), 128)

    def af(k, on, name, buf, to):
        if on:
            for j in (1, 3):
                recv((name, k, j), buf.at[half(k, c), pl.ds(256 * (4 - j), 256)])
                send((name + "f", k, j), buf.at[fwd_half(k, j), pl.ds(256 * (4 - j), 256)], buf.at[fwd_half(k, j), pl.ds(512, 256)], to(j))

    def afx(k):
        af(k, FWD_XG, "xg", dcat, lambda j: dev(dx=j))

    def afy(k):
        af(k, FWD_YG, "yg", hid, lambda j: dev(dy=j))

    def gathered(k, on, name, buf):
        if on:
            for j in (1, 3):
                recv((name + "f", k, j), buf.at[fwd_half(k, j), pl.ds(512, 256)])
        else:
            for j in (1, 3, 2):
                recv((name, k, j), buf.at[half(k, c), pl.ds(256 * (4 - j), 256)])

    def a3(k):
        gathered(k, FWD_XG, "xg", dcat)
        send(("cg", k), dcat.at[half(k, c), :], dcat.at[half(k, c), :], dev(dc=1))

    def a4(k):
        gathered(k, FWD_YG, "yg", hid)
        send(("ch", k), hid.at[half(k, c), :], hid.at[half(k, c), :], dev(dc=1))

    def need_d(k):
        recv(("cg", k), dcat.at[half(k, 1 - c), :])

    def times_w(lhs, n):
        return lax.dot_general(
            lhs, wcat[pl.ds(al(n * 256, 256), 256), :], (((1,), (1,)), ((), ())), preferred_element_type=F32
        )

    def xk(k):
        need_d(k)
        if k in DZ:
            n_k = DZ.index(k)

            @pl.loop(0, 3)
            def _(n):
                at = pl.ds(al(n * 256, 256), 256)
                part = times_w(jnp.concatenate([dcat[half(k, 1 - l), :], dcat[half(k, l), :]], axis=0), n)
                dzs[k, :, at] = part[:256].astype(BF16)
                dxo[n_k, :, at] = part[256:]

            send(("dz", k), dzs.at[k], dzr.at[k], lpart())
        else:
            n_k = DY.index(k)

            @pl.loop(0, 3)
            def _(n):
                at = pl.ds(al(n * 256, 256), 256)
                part = times_w(dcat[pl.ds(512 * k, 512), :], n).reshape(2, 4, 64, 256)
                dxs[k, :, :, :, at] = part.astype(BF16)
                dxf[n_k, :, :, :, at] = part

            for m in (2, 1, 3):
                send(("dx", k, m), dxs.at[k, :, (y + m) % 4], dxr.at[k, m - 1], dev(dy=m))

    def x2(k):
        if k in DZ:
            n_k = DZ.index(k)
            recv(("dz", k), dzr.at[k])

            @pl.loop(0, 4)
            def _(r):
                at = pl.ds(al(r * 64, 64), 64)
                total = dxo[n_k, at, :] + dzr[k, at, :].astype(F32)
                dxo[n_k, at, :] = total
                dxs[k, 0, r] = total.astype(BF16)

            for m in (2, 1, 3):
                send(("dx", k, m), dxs.at[k, 0, (y + m) % 4], dxr.at[k, m - 1, 0], dev(dy=m))
        else:
            n_k = DY.index(k)
            for m in (1, 3, 2):
                recv(("dx", k, m), dxr.at[k, m - 1])
            total = (dxf[n_k, :, y] + dxr[k, 0].astype(F32)) + (dxr[k, 1].astype(F32) + dxr[k, 2].astype(F32))
            dxf[n_k, :, 0] = total
            dxs[k, :, y] = total.astype(BF16)
            send(("dz", k), dxs.at[k, 1 - l, y], dzr.at[k, 0:64], lpart())

    def xt(k):
        at = pl.ds(64 * k, 64)
        if k in DZ:
            for m in (1, 3, 2):
                recv(("dx", k, m), dxr.at[k, m - 1, 0])
            d_in[at, :] = (
                (dxo[DZ.index(k), pl.ds(al(y * 64, 64), 64), :] + dxr[k, 0, 0].astype(F32))
                + (dxr[k, 1, 0].astype(F32) + dxr[k, 2, 0].astype(F32))
            ).astype(BF16)
        else:
            recv(("dz", k), dzr.at[k, 0:64])
            d_in[at, :] = (dxf[DY.index(k), l, 0] + dzr[k, 0:64].astype(F32)).astype(BF16)

    def grad_part(k, n, cols):
        at = pl.ds(al(n * 256, 256), 256)
        return at, lax.dot_general(
            xin[pl.ds(512 * k, 512), at], dcat[pl.ds(512 * k, 512), cols], (((0,), (0,)), ((), ())),
            preferred_element_type=F32,
        )

    begun = []

    def gp(k):
        need_d(k)
        first = not begun
        begun.append(k)

        @pl.loop(0, 3)
        def _(n):
            @pl.loop(0, 4)
            def _(j):
                cols = pl.ds(al(j * 256, 256), 256)
                at, part = grad_part(k, n, cols)
                gacc[at, cols] = part if first else gacc[at, cols] + part

    def gf(j):
        need_d(3)
        cols = pl.ds(256 * j, 256)

        @pl.loop(0, 3)
        def _(n):
            at, part = grad_part(3, n, cols)
            gs[j, at, :] = (gacc[at, cols] + part).astype(BF16)

        here = pl.ds(al(x * 768, 256), 768)
        for q, out in enumerate((g_gate, g_up)):
            src = gs.at[j, :, pl.ds(128 * q, 128)]
            if j:
                send(("gw", j, q), src, out.at[here, :], dev(dx=j))
            else:
                move(src, out.at[here, :])

    def gd():
        for k in range(4):
            recv(("ch", k), hid.at[half(k, 1 - c), :])

        @pl.loop(0, 4)
        def _(m):
            there = (y + m) % 4
            g_down[pl.ds(al(there * 256, 256), 256), :] = lax.dot_general(
                hid[:, pl.ds(al(m * 256, 256), 256)], og[...].reshape(2048, 384), (((0,), (0,)), ((), ())),
                preferred_element_type=F32,
            ).astype(BF16)

    steps = (
        (st_w, 1), (sty, 0), (st_w, 0), (st_og,), (stz, 1), (fw, 1), (sty, 3), (stz, 2), (sty, 1), (stz, 3),
        (stz, 0), (sty, 2), (fw, 0), (ox, 0), (fi, 1), (fz, 1), (fi, 0), (fw, 3), (ox, 1), (fw, 2), (b1, 0),
        (fz, 0), (ox, 2), (g1, 0), (fi, 2), (b2, 0), (g2, 0), (b1, 1), (fz, 2), (b1, 2), (g1, 1), (b2, 1),
        (ox, 3), (g3, 0), (g2, 1), (b3, 0), (g1, 2), (fi, 3), (b2, 2), (b3, 1), (b1, 3), (g2, 2), (fz, 3),
        (e, 0), (g1, 3), (b2, 3), (g3, 1), (a2y, 0), (a2x, 0), (g3, 2), (e, 1), (b3, 2), (g2, 3), (a2x, 1),
        (b3, 3), (a2y, 1), (e, 2), (afy, 0), (g3, 3), (afx, 0), (a3, 0), (a2y, 2), (a2x, 2), (afx, 1), (e, 3),
        (afy, 1), (gp, 0), (afx, 2), (a3, 1), (afy, 2), (a4, 1), (a2y, 3), (a2x, 3), (xk, 1), (xk, 0), (a3, 2),
        (afx, 3), (gp, 1), (a3, 3), (gp, 2), (afy, 3), (gf, 3), (xk, 3), (gf, 2), (xk, 2), (a4, 0), (a4, 3),
        (a4, 2), (gd,), (gf, 1), (x2, 0), (x2, 3), (x2, 2), (x2, 1), (xt, 1), (xt, 3), (gf, 0), (xt, 0), (xt, 2),
    )
    for step in steps:
        step[0](*step[1:])

    for j in (1, 3, 2):
        for q, out in enumerate((g_gate, g_up)):
            recv(("gw", j, q), out.at[pl.ds(al(((x - j + 4) % 4) * 768, 256), 768), :])
    for copy in local[n_first:]:
        copy.wait()
    done = [id(copy) for copy in uses[:-N_SLOT]]
    for copy in sent:
        if id(copy) not in done:
            copy.wait_send()
    assert len(index) <= N_SEM, len(index)


def shards(inputs, out_grad, w_gate, w_up, w_down):
    v = pltpu.VMEM
    any_ = pl.BlockSpec(memory_space=pl.ANY)
    vm = pl.BlockSpec(memory_space=pltpu.VMEM)
    return pl.pallas_call(
        kernel,
        name="swiglu_back",
        out_shape=(
            jax.ShapeDtypeStruct((256, 768), BF16),
            jax.ShapeDtypeStruct((3072, 128), BF16),
            jax.ShapeDtypeStruct((3072, 128), BF16),
            jax.ShapeDtypeStruct((1024, 384), BF16),
        ),
        in_specs=[any_] * 5,
        out_specs=(vm, any_, any_, vm),
        scratch_shapes=[
            v((2048, 768), BF16),
            v((768, 1024), BF16),
            v((4, 8, 64, 384), BF16),
            v((1024, 384), BF16),
            v((N_SLOT, 512, 1024), F32),
            v((8, 256, 1024), F32),
            v((8, 256, 1024), BF16),
            v((4, 3, 256, 256), BF16),
            v((4, 3, 256, 256), BF16),
            v((4, 256, 256), F32),
            v((4, 128, 256), F32),
            v((4, 256, 256), F32),
            v((4, 3, 128, 128), F32),
            v((2048, 1024), BF16),
            v((2048, 1024), BF16),
            v((4, 256, 768), BF16),
            v((4, 256, 768), BF16),
            v((max(1, len(DZ)), 256, 768), F32),
            v((max(1, len(DY)), 2, 4, 64, 768), F32),
            v((4, 2, 4, 64, 768), BF16),
            v((4, 3, 2, 64, 768), BF16),
            v((4, 768, 256), BF16),
            v((768, 1024), F32),
            pltpu.SemaphoreType.DMA((N_SEM,)),
            pltpu.SemaphoreType.DMA((N_SEM,)),
            pltpu.SemaphoreType.DMA((16,)),
        ],
        compiler_params=pltpu.CompilerParams(collective_id=0, has_side_effects=True, vmem_limit_bytes=61 * 2**20),
        cost_estimate=pl.CostEstimate(flops=13 * 10**9, bytes_accessed=8 * 2**20, transcendentals=65536),
    )(inputs, out_grad.reshape(4, 4, 16, 3072), w_gate, w_up, w_down)


def solution(mesh):
    in_specs = (
        P("tok", "in"),
        P("tok", "in"),
        P("in", ("out", "tok")),
        P("in", ("out", "tok")),
        P("out", ("in", "tok")),
    )
    out_specs = (
        P("tok", ("in", "out")),
        P("in", ("out", "tok")),
        P("in", ("out", "tok")),
        P("out", ("in", "tok")),
    )
    return jax.shard_map(shards, mesh=mesh, in_specs=in_specs, out_specs=out_specs, check_vma=False)
```

time: 195 us -> 132 us (0.68); the launches traced: 192 us -> 132 us
  Pallas kernels: 186 us -> 125 us
    pallas_call x1, Pallas kernels: 186 us -> 125 us  [shards(): pl.pallas_call(kernel, name='swiglu_back', out_shape=(jax.ShapeDtypeStruc...]
where the time goes in v2:
time: 132 us
  Pallas kernels  125 us (95%)
  local copies, waits for them, and re-layouts  5.74 us (4%)
    pallas_call x1, Pallas kernels, shards(): pl.pallas_call(kernel, name='swiglu_back', out_shape=(jax.ShapeDtypeStruc...  125 us
    unnamed x8, local copies, waits for them, and re-layouts  5.74 us

profile of v2, /device:TPU:1, one launch (start us, length us, event | category | flops | bytes accessed | tf_op | source)
XLA Modules:
  0.0 131.6 jit_solution(14369145589951207859)
XLA Ops:
  0.6 125.2 %swiglu_back.1 = (bf16[256,768]{1,0:T(8,128)(2,1)}, bf16[3072,128]{1,0:T(8,128)(2,1)}, bf16[3072,128]{1,0:T(8,128)(2,1)}, bf16[1024,384]{1,0:T(8,128)(2,1)}) custom-call(bf16[256,3072]{1,0:T(8,128)(2,1)} %inputs.1, bf16[4,4,16,3072]{3,2,1,0:T(8,128)(2,1)} %bitcast.1, bf16[3072,128]{1,0:T(8,128)(2,1)} %w_gate.1, bf16[3072,128]{1,0:T(8,128)(2,1)} %w_up.1, ...), custom_call_target="tpu_custom_call" | custom-call | flops 12999999488 | bytes 8388608 | tf_op jit(solution)/shard_map/swiglu_back/pallas_call | solution.py:518
  125.8 0.0 copy-start.1
  125.9 1.8 %copy.13 = bf16[256,768]{1,0:T(8,128)(2,1)} copy(bf16[256,768]{1,0:T(8,128)(2,1)} %get-tuple-element.8) | data formatting | bytes 786432
  127.7 0.0 copy-start
  127.7 2.1 %copy.14 = bf16[3072,128]{1,0:T(8,128)(2,1)} copy(bf16[3072,128]{1,0:T(8,128)(2,1)} %get-tuple-element.9) | data formatting | bytes 1572864
  129.8 0.0 copy-done.1
  129.8 0.9 copy.15
  130.7 0.0 copy-done
  130.7 0.9 copy.16
Async XLA Ops:
  125.8 4.0 %copy-start.1 = (bf16[3072,128]{1,0:T(8,128)(2,1)S(1)}, bf16[3072,128]{1,0:T(8,128)(2,1)}, u32[]{:S(2)}) copy-start(bf16[3072,128]{1,0:T(8,128)(2,1)} %get-tuple-element.10) | copy-start | bytes 2359300
  127.7 3.0 %copy-start = (bf16[1024,384]{1,0:T(8,128)(2,1)S(1)}, bf16[1024,384]{1,0:T(8,128)(2,1)}, u32[]{:S(2)}) copy-start(bf16[1024,384]{1,0:T(8,128)(2,1)} %get-tuple-element.11) | copy-start | bytes 2359300

commit v3 on v2

--- a/solution.py
+++ b/solution.py
@@ -511,11 +511,27 @@
     assert len(index) <= N_SEM, len(index)
 
 
+def finish(*refs):
+    ins, outs = [], []
+    for k, (src, dst) in enumerate(zip(refs[:4], refs[4:8])):
+        buf, n = refs[8 + k], src.shape[0] // 4
+        for part in range(4):
+            at = pl.ds(part * n, n)
+            ins.append(pltpu.make_async_copy(src.at[at], buf.at[at], refs[12].at[len(ins)]))
+            outs.append(pltpu.make_async_copy(buf.at[at], dst.at[at], refs[13].at[len(outs)]))
+            ins[-1].start()
+    for first, then in zip(ins, outs):
+        first.wait()
+        then.start()
+    for then in outs:
+        then.wait()
+
+
 def shards(inputs, out_grad, w_gate, w_up, w_down):
     v = pltpu.VMEM
     any_ = pl.BlockSpec(memory_space=pl.ANY)
     vm = pl.BlockSpec(memory_space=pltpu.VMEM)
-    return pl.pallas_call(
+    outs = pl.pallas_call(
         kernel,
         name="swiglu_back",
         out_shape=(
@@ -557,6 +573,15 @@
         compiler_params=pltpu.CompilerParams(collective_id=0, has_side_effects=True, vmem_limit_bytes=61 * 2**20),
         cost_estimate=pl.CostEstimate(flops=13 * 10**9, bytes_accessed=8 * 2**20, transcendentals=65536),
     )(inputs, out_grad.reshape(4, 4, 16, 3072), w_gate, w_up, w_down)
+    return pl.pallas_call(
+        finish,
+        name="results",
+        out_shape=tuple(jax.ShapeDtypeStruct(v.shape, v.dtype) for v in outs),
+        in_specs=[any_] * 4,
+        out_specs=(any_,) * 4,
+        scratch_shapes=[v(o.shape, o.dtype) for o in outs] + [pltpu.SemaphoreType.DMA((16,))] * 2,
+        cost_estimate=pl.CostEstimate(flops=0, bytes_accessed=5 * 2**20, transcendentals=0),
+    )(*outs)
 
 
 def solution(mesh):

time: 132 us -> 129 us (0.977)
  local copies, waits for them, and re-layouts: 5.74 us -> 0 us
  Pallas kernels: 125 us -> 128 us
    unnamed x8 -> x0, local copies, waits for them, and re-layouts: 5.74 us -> none
    pallas_call x0 -> x1, Pallas kernels: none -> 2.82 us  [shards(): pl.pallas_call(finish, name='results', out_shape=tuple((jax.ShapeDtypeStr...]
where the time goes in v3:
time: 129 us
  Pallas kernels  128 us (99%)
    pallas_call x1, Pallas kernels, shards(): pl.pallas_call(kernel, name='swiglu_back', out_shape=(jax.ShapeDtypeStruc...  125 us
    pallas_call x1, Pallas kernels, shards(): pl.pallas_call(finish, name='results', out_shape=tuple((jax.ShapeDtypeStr...  2.82 us

profile of v3, /device:TPU:1, one launch (start us, length us, event | category | flops | bytes accessed | tf_op | source)
XLA Modules:
  0.0 128.6 jit_solution(15384740946244045357)
XLA Ops:
  0.6 125.2 %swiglu_back.1 = (bf16[256,768]{1,0:T(8,128)(2,1)}, bf16[3072,128]{1,0:T(8,128)(2,1)}, bf16[3072,128]{1,0:T(8,128)(2,1)}, bf16[1024,384]{1,0:T(8,128)(2,1)}) custom-call(bf16[256,3072]{1,0:T(8,128)(2,1)} %inputs.1, bf16[4,4,16,3072]{3,2,1,0:T(8,128)(2,1)} %bitcast.1, bf16[3072,128]{1,0:T(8,128)(2,1)} %w_gate.1, bf16[3072,128]{1,0:T(8,128)(2,1)} %w_up.1, ...), custom_call_target="tpu_custom_call" | custom-call | flops 12999999488 | bytes 8388608 | tf_op jit(solution)/shard_map/swiglu_back/pallas_call | solution.py:534
  125.8 2.8 %results.1 = (bf16[256,768]{1,0:T(8,128)(2,1)}, bf16[3072,128]{1,0:T(8,128)(2,1)}, bf16[3072,128]{1,0:T(8,128)(2,1)}, bf16[1024,384]{1,0:T(8,128)(2,1)}) custom-call(bf16[256,768]{1,0:T(8,128)(2,1)} %get-tuple-element.8.refs_0_, bf16[3072,128]{1,0:T(8,128)(2,1)} %get-tuple-element.9.refs_1_, bf16[3072,128]{1,0:T(8,128)(2,1)} %get-tuple-element.10.refs_2_, ...), custom_call_target="tpu_custom_call" | custom-call | bytes 5242880 | tf_op jit(solution)/shard_map/results/pallas_call | solution.py:576

commit v4 on v3

--- a/solution.py
+++ b/solution.py
@@ -10,7 +10,8 @@
 BF16 = jnp.bfloat16
 N_SEM = 230
 N_SLOT = 3
-DZ = (0, 2)
+OX = (2, 4)
+DZ = (0, 2, 3)
 DY = tuple(k for k in range(4) if k not in DZ)
 Z_FIRST = (0, 1, 2, 3)
 FWD_IN, FWD_XG, FWD_YG, FWD_OG = True, False, True, False
@@ -19,7 +20,7 @@
 def kernel(
     inputs, out_grad, w_gate, w_up, w_down,
     d_in, g_gate, g_up, g_down,
-    xin, wcat, og, wdn, pbuf, pr, s2, xr, yr, zg, zgr, zb, zbr, dcat, hid, dzs, dzr, dxo, dxf, dxs, dxr, gs, gacc,
+    xin, wcat, og, wdn, pbuf, pr, s2, xr, yr, zg, zgr, zb, zbr, yb, dcat, hid, dzs, dzr, dxo, dxf, dxs, dxr, gs, gacc,
     ssem, rsem, lsem,
 ):
     i = lax.axis_index("in")
@@ -78,12 +79,17 @@
         return pl.ds(al(s * 512 + part * 256, 256), 256)
 
     cols_in = pl.ds(al(x * 768, 128), 768)
-    mine16 = pl.ds(al(x * 16, 16), 16)
+    by_x = pl.ds(OX[0], OX[1] - OX[0])
     own_in = []
     for s in range(4):
         here = pl.ds(64 * s, 64)
         own_in.append(move(inputs.at[here, cols_in], xin.at[rows(s, y, l), :]))
-    own_og = move(out_grad.at[:, x, :, pl.ds(al(t * 384, 128), 384)], og.at[:, 4 * l + y, mine16, :])
+    own_og = {}
+    for s in range(4):
+        if not OX[0] <= s < OX[1]:
+            own_og[s] = move(out_grad.at[s, :, :, pl.ds(al(t * 384, 128), 384)], og.at[s, 4 * l + y])
+    if OX[0] < OX[1]:
+        own_og[-1] = move(out_grad.at[by_x, x, :, pl.ds(al(t * 384, 128), 384)], og.at[by_x, 4 * l + y, x])
     own_dn = move(w_down, wdn)
     own_w = [
         move(w.at[pl.ds(al(x * 768, 256), 768), :], wcat.at[:, pl.ds(128 * q, 128)])
@@ -105,41 +111,55 @@
     def og_cols(yy, ll):
         return pl.ds(al((2 * yy + ll) * 384, 128), 384)
 
-    def st_og():
-        send(("og", 0, 1), out_grad.at[:, x, :, og_cols(y, 1 - l)], og.at[:, 4 * l + y, mine16, :], lpart())
+    def og_from(s, yy, ll):
+        return og.at[s, 4 * ll + yy] if s >= 0 else og.at[by_x, 4 * ll + yy, x]
+
+    def og_src(s, yy, ll):
+        return out_grad.at[s, :, :, og_cols(yy, ll)] if s >= 0 else out_grad.at[by_x, x, :, og_cols(yy, ll)]
+
+    def st_og(s):
+        send(("og", s, 0, 1), og_src(s, y, 1 - l), og_from(s, y, l), lpart())
         for m in (2, 1, 3):
             there = (y + m) % 4
-            send(("og", m, 0), out_grad.at[:, x, :, og_cols(there, l)], og.at[:, 4 * l + y, mine16, :], dev(dy=m))
-            send(("og", m, 1), out_grad.at[:, x, :, og_cols(there, 1 - l)], og.at[:, 4 * l + y, mine16, :], cross[m - 1])
-
-    def take_og():
-        own_og.wait()
-        recv(("og", 0, 1), og.at[:, 4 * (1 - l) + y, mine16, :])
+            send(("og", s, m, 0), og_src(s, there, l), og_from(s, y, l), dev(dy=m))
+            send(("og", s, m, 1), og_src(s, there, 1 - l), og_from(s, y, l), cross[m - 1])
+
+    def take_og(s):
+        if s not in taken:
+            own_og[s].wait()
+            taken.append(s)
+        recv(("og", s, 0, 1), og_from(s, y, 1 - l))
         for m in (1, 3, 2):
             yy = (y - m + 4) % 4
-            recv(("og", m, 0), og.at[:, 4 * l + yy, mine16, :])
-            recv(("og", m, 1), og.at[:, 4 * (1 - l) + yy, mine16, :])
-
-    def og_part(s, j, lo=0, n=16):
-        return og.at[s, :, pl.ds(al(((x + j) % 4) * 16 + lo, n), n), :]
+            recv(("og", s, m, 0), og_from(s, yy, l))
+            recv(("og", s, m, 1), og_from(s, yy, 1 - l))
+
+    taken = []
+
+    def og_part(s, j):
+        return og.at[s, :, (x + j) % 4]
 
     def ox(s):
-        if s == 0:
-            take_og()
-        for j in (1, 3) if FWD_OG else (2, 1, 3):
-            send(("ox", s, j), og_part(s, 0), og_part(s, 0), dev(dx=j))
+        if OX[0] <= s < OX[1]:
+            take_og(-1)
+            for j in (1, 3) if FWD_OG else (2, 1, 3):
+                send(("ox", s, j), og_part(s, 0), og_part(s, 0), dev(dx=j))
+
+    def og_far(s, j):
+        return og.at[s, pl.ds(0 if j == 1 else 4, 4), (x - j + 4) % 4]
 
     def fo(s):
-        if FWD_OG:
+        if FWD_OG and OX[0] <= s < OX[1]:
             for j in (1, 3):
-                part = og.at[s, pl.ds(0 if j == 1 else 4, 4), pl.ds(al(((x - j + 4) % 4) * 16, 16), 16), :]
                 recv(("ox", s, j), og_part(s, 4 - j))
-                send(("of", s, j), part, part, dev(dx=j))
+                send(("of", s, j), og_far(s, j), og_far(s, j), dev(dx=j))
 
     def wait_og(s):
-        if FWD_OG:
+        if not OX[0] <= s < OX[1]:
+            take_og(s)
+        elif FWD_OG:
             for j in (1, 3):
-                recv(("of", s, j), og.at[s, pl.ds(0 if j == 1 else 4, 4), pl.ds(al(((x + 2) % 4) * 16, 16), 16), :])
+                recv(("of", s, j), og.at[s, pl.ds(0 if j == 1 else 4, 4), (x + 2) % 4])
         else:
             for j in (1, 3, 2):
                 recv(("ox", s, j), og_part(s, 4 - j))
@@ -229,24 +249,28 @@
 
     def b1(s):
         wait_og(s)
-        if s == 0:
+        if "dn" not in taken:
             own_dn.wait()
+            taken.append("dn")
         slot = partial_slot()
         slots["b", s] = slot
 
         @pl.loop(0, 4)
         def _(m):
             there = (y + m) % 4
-            pbuf[slot, :, pl.ds(al(m * 256, 256), 256)] = lax.dot_general(
+            part = lax.dot_general(
                 og[s].reshape(512, 384), wdn[pl.ds(al(there * 256, 256), 256), :],
                 (((1,), (1,)), ((), ())), preferred_element_type=F32,
             )
+            for ll in (0, 1):
+                pbuf[slot, :, pl.ds(al(ll * 512 + m * 128, 128), 128)] = part[:, 128 * ll : 128 * ll + 128]
 
         core_send(slot, 4 + s)
 
     def g1(s):
         wait_in(s)
-        if s == 0:
+        if "w" not in taken:
+            taken.append("w")
             for copy in own_w:
                 copy.wait()
             for j in (1, 3, 2):
@@ -275,8 +299,10 @@
 
     def b2(s):
         core_sum(slots["b", s], 4 + s)
-        for m in (2, 1, 3):
-            send(("yr", s, m), s2.at[4 + s, :, pl.ds(256 * m, 256)], yr.at[s, m - 1], dev(dy=m))
+        for d in (2, 1, 3):
+            zz = (z + d) % 4
+            at = (4 + s, pl.ds(al((zz // 2) * 128, 128), 128), pl.ds(al((zz % 2) * 512, 512), 512))
+            send(("zb", s, d), s2.at[at], zbr.at[s, d - 1], dev(dz=d))
 
     def g2(s):
         core_sum(slots["g", s], s)
@@ -284,15 +310,14 @@
             send(("xr", s, j), s2.at[s, :, pl.ds(256 * j, 256)], xr.at[s, j - 1], dev(dx=j))
 
     def b3(k):
-        for m in (1, 3, 2):
-            recv(("yr", k, m), yr.at[k, m - 1])
-        zb[k] = (pr[4 + k, :, 0:256] + yr[k, 0].astype(F32)) + (yr[k, 1].astype(F32) + yr[k, 2].astype(F32))
-        for d in (2, 1, 3):
-            zz = (z + d) % 4
-            send(
-                ("zb", k, d), zb.at[k, pl.ds(al((zz // 2) * 128, 128), 128), pl.ds(al((zz % 2) * 128, 128), 128)],
-                zbr.at[k, d - 1], dev(dz=d),
-            )
+        for d in (1, 3, 2):
+            recv(("zb", k, d), zbr.at[k, d - 1])
+        mine = pr[4 + k, pl.ds(al(h * 128, 128), 128), pl.ds(al(l * 512, 512), 512)]
+        total = (mine + zbr[k, 0].astype(F32)) + (zbr[k, 1].astype(F32) + zbr[k, 2].astype(F32))
+        zb[k] = total[:, :128]
+        yb[k] = total.astype(BF16)
+        for m in (2, 1, 3):
+            send(("yr", k, m), yb.at[k, :, pl.ds(128 * m, 128)], yr.at[k, m - 1], dev(dy=m))
 
     def g3(k):
         for j in (1, 3, 2):
@@ -302,12 +327,12 @@
 
     def e(k):
         recv(("zg", k), zgr.at[k])
-        for d in (1, 2, 3):
-            recv(("zb", k, d), zbr.at[k, d - 1])
+        for m in (1, 3, 2):
+            recv(("yr", k, m), yr.at[k, m - 1])
         mine = pl.ds(al(h * 128, 128), 128)
         both = zg[k, mine, :] + zgr[k]
         gate, up = both[:, :128], both[:, 128:]
-        back = (zb[k, mine, pl.ds(al(l * 128, 128), 128)] + zbr[k, 0]) + (zbr[k, 1] + zbr[k, 2])
+        back = (zb[k] + yr[k, 0].astype(F32)) + (yr[k, 1].astype(F32) + yr[k, 2].astype(F32))
         sig = jax.nn.sigmoid(gate)
         act = gate * sig
         at = pl.ds(al(k * 512 + c * 256 + h * 128, 128), 128)
@@ -486,15 +511,15 @@
             ).astype(BF16)
 
     steps = (
-        (st_w, 1), (sty, 0), (st_w, 0), (st_og,), (stz, 1), (fw, 1), (sty, 3), (stz, 2), (sty, 1), (stz, 3),
-        (stz, 0), (sty, 2), (fw, 0), (ox, 0), (fi, 1), (fz, 1), (fi, 0), (fw, 3), (ox, 1), (fw, 2), (b1, 0),
-        (fz, 0), (ox, 2), (g1, 0), (fi, 2), (b2, 0), (g2, 0), (b1, 1), (fz, 2), (b1, 2), (g1, 1), (b2, 1),
-        (ox, 3), (g3, 0), (g2, 1), (b3, 0), (g1, 2), (fi, 3), (b2, 2), (b3, 1), (b1, 3), (g2, 2), (fz, 3),
-        (e, 0), (g1, 3), (b2, 3), (g3, 1), (a2y, 0), (a2x, 0), (g3, 2), (e, 1), (b3, 2), (g2, 3), (a2x, 1),
-        (b3, 3), (a2y, 1), (e, 2), (afy, 0), (g3, 3), (afx, 0), (a3, 0), (a2y, 2), (a2x, 2), (afx, 1), (e, 3),
-        (afy, 1), (gp, 0), (afx, 2), (a3, 1), (afy, 2), (a4, 1), (a2y, 3), (a2x, 3), (xk, 1), (xk, 0), (a3, 2),
-        (afx, 3), (gp, 1), (a3, 3), (gp, 2), (afy, 3), (gf, 3), (xk, 3), (gf, 2), (xk, 2), (a4, 0), (a4, 3),
-        (a4, 2), (gd,), (gf, 1), (x2, 0), (x2, 3), (x2, 2), (x2, 1), (xt, 1), (xt, 3), (gf, 0), (xt, 0), (xt, 2),
+        (stz, 1), (sty, 1), (st_w, 0), (st_og, -1), (sty, 0), (st_w, 1), (st_og, 1), (stz, 3), (fw, 1), (stz, 0),
+        (ox, 2), (st_og, 0), (fw, 0), (b1, 1), (stz, 2), (fi, 1), (b2, 1), (sty, 3), (ox, 3), (b1, 0), (fi, 0),
+        (sty, 2), (g1, 1), (b2, 0), (fw, 2), (b1, 2), (g2, 1), (fw, 3), (g1, 0), (fi, 2), (g2, 0), (b2, 2),
+        (fi, 3), (b3, 1), (g1, 2), (g3, 1), (g2, 2), (g3, 0), (b3, 0), (g1, 3), (e, 1), (e, 0), (g2, 3), (b1, 3),
+        (g3, 2), (a2y, 1), (b2, 3), (a2x, 0), (b3, 2), (e, 2), (afy, 1), (a2x, 1), (g3, 3), (b3, 3), (a3, 0),
+        (a2x, 2), (e, 3), (a3, 1), (a2y, 2), (xk, 0), (a2y, 0), (a3, 2), (a2y, 3), (a2x, 3), (xk, 1), (xk, 2),
+        (gp, 1), (gp, 2), (a3, 3), (gp, 0), (a4, 1), (afy, 3), (afy, 0), (gf, 2), (afy, 2), (xk, 3), (gf, 3),
+        (x2, 0), (gf, 1), (x2, 2), (a4, 3), (a4, 2), (a4, 0), (gd,), (x2, 1), (x2, 3), (gf, 0), (xt, 0), (xt, 1),
+        (xt, 2), (xt, 3),
     )
     for step in steps:
         step[0](*step[1:])
@@ -545,17 +570,18 @@
         scratch_shapes=[
             v((2048, 768), BF16),
             v((768, 1024), BF16),
-            v((4, 8, 64, 384), BF16),
+            v((4, 8, 4, 16, 384), BF16),
             v((1024, 384), BF16),
             v((N_SLOT, 512, 1024), F32),
             v((8, 256, 1024), F32),
             v((8, 256, 1024), BF16),
             v((4, 3, 256, 256), BF16),
-            v((4, 3, 256, 256), BF16),
+            v((4, 3, 128, 128), BF16),
             v((4, 256, 256), F32),
             v((4, 128, 256), F32),
-            v((4, 256, 256), F32),
-            v((4, 3, 128, 128), F32),
+            v((4, 128, 128), F32),
+            v((4, 3, 128, 512), BF16),
+            v((4, 128, 512), BF16),
             v((2048, 1024), BF16),
             v((2048, 1024), BF16),
             v((4, 256, 768), BF16),
@@ -568,7 +594,7 @@
             v((768, 1024), F32),
             pltpu.SemaphoreType.DMA((N_SEM,)),
             pltpu.SemaphoreType.DMA((N_SEM,)),
-            pltpu.SemaphoreType.DMA((16,)),
+            pltpu.SemaphoreType.DMA((20,)),
         ],
         compiler_params=pltpu.CompilerParams(collective_id=0, has_side_effects=True, vmem_limit_bytes=61 * 2**20),
         cost_estimate=pl.CostEstimate(flops=13 * 10**9, bytes_accessed=8 * 2**20, transcendentals=65536),

time: 129 us -> 123 us (0.953)
  Pallas kernels: 128 us -> 123 us
    pallas_call x1, Pallas kernels: 125 us -> 120 us  [shards(): pl.pallas_call(kernel, name='swiglu_back', out_shape=(jax.ShapeDtypeStruc...]
where the time goes in v4:
time: 123 us
  Pallas kernels  123 us (100%)
    pallas_call x1, Pallas kernels, shards(): pl.pallas_call(kernel, name='swiglu_back', out_shape=(jax.ShapeDtypeStruc...  120 us
    pallas_call x1, Pallas kernels, shards(): pl.pallas_call(finish, name='results', out_shape=tuple((jax.ShapeDtypeStr...  2.82 us

profile of v4, /device:TPU:1, one launch (start us, length us, event | category | flops | bytes accessed | tf_op | source)
XLA Modules:
  0.0 123.3 jit_solution(11279499716214567753)
XLA Ops:
  0.6 119.9 %swiglu_back.1 = (bf16[256,768]{1,0:T(8,128)(2,1)}, bf16[3072,128]{1,0:T(8,128)(2,1)}, bf16[3072,128]{1,0:T(8,128)(2,1)}, bf16[1024,384]{1,0:T(8,128)(2,1)}) custom-call(bf16[256,3072]{1,0:T(8,128)(2,1)} %inputs.1, bf16[4,4,16,3072]{3,2,1,0:T(8,128)(2,1)} %bitcast.1, bf16[3072,128]{1,0:T(8,128)(2,1)} %w_gate.1, bf16[3072,128]{1,0:T(8,128)(2,1)} %w_up.1, ...), custom_call_target="tpu_custom_call" | custom-call | flops 12999999488 | bytes 8388608 | tf_op jit(solution)/shard_map/swiglu_back/pallas_call | solution.py:559
  120.5 2.8 %results.1 = (bf16[256,768]{1,0:T(8,128)(2,1)}, bf16[3072,128]{1,0:T(8,128)(2,1)}, bf16[3072,128]{1,0:T(8,128)(2,1)}, bf16[1024,384]{1,0:T(8,128)(2,1)}) custom-call(bf16[256,768]{1,0:T(8,128)(2,1)} %get-tuple-element.8.refs_0_, bf16[3072,128]{1,0:T(8,128)(2,1)} %get-tuple-element.9.refs_1_, bf16[3072,128]{1,0:T(8,128)(2,1)} %get-tuple-element.10.refs_2_, ...), custom_call_target="tpu_custom_call" | custom-call | bytes 5242880 | tf_op jit(solution)/shard_map/results/pallas_call | solution.py:602

commit v5 on v4

--- a/solution.py
+++ b/solution.py
@@ -12,6 +12,7 @@
 N_SLOT = 3
 OX = (2, 4)
 DZ = (0, 2, 3)
+TILED = (3,)
 DY = tuple(k for k in range(4) if k not in DZ)
 Z_FIRST = (0, 1, 2, 3)
 FWD_IN, FWD_XG, FWD_YG, FWD_OG = True, False, True, False
@@ -399,7 +400,14 @@
 
     def xk(k):
         need_d(k)
-        if k in DZ:
+        if k in TILED:
+            for n in range(3):
+                at = pl.ds(256 * n, 256)
+                part = times_w(jnp.concatenate([dcat[half(k, 1 - l), :], dcat[half(k, l), :]], axis=0), n)
+                dzs[k, :, at] = part[:256].astype(BF16)
+                send(("dz", k, n), dzs.at[k, :, at], dzr.at[k, :, at], lpart())
+                dxo[DZ.index(k), :, at] = part[256:]
+        elif k in DZ:
             n_k = DZ.index(k)
 
             @pl.loop(0, 3)
@@ -424,7 +432,19 @@
                 send(("dx", k, m), dxs.at[k, :, (y + m) % 4], dxr.at[k, m - 1], dev(dy=m))
 
     def x2(k):
-        if k in DZ:
+        if k in TILED:
+            n_k = DZ.index(k)
+            for n in range(3):
+                cols = pl.ds(256 * n, 256)
+                recv(("dz", k, n), dzr.at[k, :, cols])
+                total = dxo[n_k, :, cols] + dzr[k, :, cols].astype(F32)
+                dxo[n_k, :, cols] = total
+                dxs[k, 0, :, :, cols] = total.astype(BF16).reshape(4, 64, 256)
+                for m in (2, 1, 3):
+                    send(
+                        ("dx", k, m, n), dxs.at[k, 0, (y + m) % 4, :, cols], dxr.at[k, m - 1, 0, :, cols], dev(dy=m)
+                    )
+        elif k in DZ:
             n_k = DZ.index(k)
             recv(("dz", k), dzr.at[k])
 
@@ -450,7 +470,11 @@
         at = pl.ds(64 * k, 64)
         if k in DZ:
             for m in (1, 3, 2):
-                recv(("dx", k, m), dxr.at[k, m - 1, 0])
+                if k in TILED:
+                    for n in range(3):
+                        recv(("dx", k, m, n), dxr.at[k, m - 1, 0, :, pl.ds(256 * n, 256)])
+                else:
+                    recv(("dx", k, m), dxr.at[k, m - 1, 0])
             d_in[at, :] = (
                 (dxo[DZ.index(k), pl.ds(al(y * 64, 64), 64), :] + dxr[k, 0, 0].astype(F32))
                 + (dxr[k, 1, 0].astype(F32) + dxr[k, 2, 0].astype(F32))
@@ -511,15 +535,15 @@
             ).astype(BF16)
 
     steps = (
-        (stz, 1), (sty, 1), (st_w, 0), (st_og, -1), (sty, 0), (st_w, 1), (st_og, 1), (stz, 3), (fw, 1), (stz, 0),
-        (ox, 2), (st_og, 0), (fw, 0), (b1, 1), (stz, 2), (fi, 1), (b2, 1), (sty, 3), (ox, 3), (b1, 0), (fi, 0),
-        (sty, 2), (g1, 1), (b2, 0), (fw, 2), (b1, 2), (g2, 1), (fw, 3), (g1, 0), (fi, 2), (g2, 0), (b2, 2),
-        (fi, 3), (b3, 1), (g1, 2), (g3, 1), (g2, 2), (g3, 0), (b3, 0), (g1, 3), (e, 1), (e, 0), (g2, 3), (b1, 3),
-        (g3, 2), (a2y, 1), (b2, 3), (a2x, 0), (b3, 2), (e, 2), (afy, 1), (a2x, 1), (g3, 3), (b3, 3), (a3, 0),
-        (a2x, 2), (e, 3), (a3, 1), (a2y, 2), (xk, 0), (a2y, 0), (a3, 2), (a2y, 3), (a2x, 3), (xk, 1), (xk, 2),
-        (gp, 1), (gp, 2), (a3, 3), (gp, 0), (a4, 1), (afy, 3), (afy, 0), (gf, 2), (afy, 2), (xk, 3), (gf, 3),
-        (x2, 0), (gf, 1), (x2, 2), (a4, 3), (a4, 2), (a4, 0), (gd,), (x2, 1), (x2, 3), (gf, 0), (xt, 0), (xt, 1),
-        (xt, 2), (xt, 3),
+        (stz, 1), (st_og, -1), (st_w, 0), (st_og, 0), (sty, 1), (fw, 1), (stz, 2), (ox, 3), (st_og, 1), (stz, 3),
+        (st_w, 1), (sty, 0), (fw, 2), (fi, 1), (stz, 0), (b1, 0), (b1, 1), (fw, 3), (b2, 0), (fw, 0), (b1, 3),
+        (sty, 2), (ox, 2), (g1, 1), (b2, 1), (b2, 3), (fi, 0), (g2, 1), (sty, 3), (fi, 2), (b1, 2), (g1, 0),
+        (fi, 3), (b2, 2), (g2, 0), (g1, 2), (b3, 1), (g3, 1), (g1, 3), (g2, 2), (g3, 0), (g2, 3), (b3, 0),
+        (e, 1), (b3, 3), (e, 0), (b3, 2), (a2x, 1), (g3, 2), (a2y, 1), (g3, 3), (a2x, 0), (e, 2), (afy, 1),
+        (a3, 1), (a2x, 2), (a2y, 2), (a2y, 0), (e, 3), (a4, 1), (a3, 0), (xk, 1), (xk, 0), (a2x, 3), (a3, 2),
+        (gp, 1), (a2y, 3), (xk, 2), (gp, 2), (a3, 3), (gp, 0), (x2, 0), (gf, 2), (afy, 0), (gf, 1), (afy, 2),
+        (afy, 3), (gf, 3), (xk, 3), (x2, 2), (a4, 3), (x2, 1), (a4, 2), (a4, 0), (x2, 3), (gd,), (xt, 2),
+        (xt, 0), (xt, 1), (gf, 0), (xt, 3),
     )
     for step in steps:
         step[0](*step[1:])

time: 123 us -> 120 us (0.976)
  Pallas kernels: 123 us -> 120 us
    pallas_call x1, Pallas kernels: 120 us -> 117 us  [shards(): pl.pallas_call(kernel, name='swiglu_back', out_shape=(jax.ShapeDtypeStruc...]
where the time goes in v5:
time: 120 us
  Pallas kernels  120 us (100%)
    pallas_call x1, Pallas kernels, shards(): pl.pallas_call(kernel, name='swiglu_back', out_shape=(jax.ShapeDtypeStruc...  117 us
    pallas_call x1, Pallas kernels, shards(): pl.pallas_call(finish, name='results', out_shape=tuple((jax.ShapeDtypeStr...  2.82 us

profile of v5, /device:TPU:1, one launch (start us, length us, event | category | flops | bytes accessed | tf_op | source)
XLA Modules:
  0.0 120.3 jit_solution(16879166403320332823)
XLA Ops:
  0.6 116.8 %swiglu_back.1 = (bf16[256,768]{1,0:T(8,128)(2,1)}, bf16[3072,128]{1,0:T(8,128)(2,1)}, bf16[3072,128]{1,0:T(8,128)(2,1)}, bf16[1024,384]{1,0:T(8,128)(2,1)}) custom-call(bf16[256,3072]{1,0:T(8,128)(2,1)} %inputs.1, bf16[4,4,16,3072]{3,2,1,0:T(8,128)(2,1)} %bitcast.1, bf16[3072,128]{1,0:T(8,128)(2,1)} %w_gate.1, bf16[3072,128]{1,0:T(8,128)(2,1)} %w_up.1, ...), custom_call_target="tpu_custom_call" | custom-call | flops 12999999488 | bytes 8388608 | tf_op jit(solution)/shard_map/swiglu_back/pallas_call | solution.py:583
  117.5 2.8 %results.1 = (bf16[256,768]{1,0:T(8,128)(2,1)}, bf16[3072,128]{1,0:T(8,128)(2,1)}, bf16[3072,128]{1,0:T(8,128)(2,1)}, bf16[1024,384]{1,0:T(8,128)(2,1)}) custom-call(bf16[256,768]{1,0:T(8,128)(2,1)} %get-tuple-element.8.refs_0_, bf16[3072,128]{1,0:T(8,128)(2,1)} %get-tuple-element.9.refs_1_, bf16[3072,128]{1,0:T(8,128)(2,1)} %get-tuple-element.10.refs_2_, ...), custom_call_target="tpu_custom_call" | custom-call | bytes 5242880 | tf_op jit(solution)/shard_map/results/pallas_call | solution.py:626

commit v6 on v5

--- a/solution.py
+++ b/solution.py
@@ -20,8 +20,8 @@
 
 def kernel(
     inputs, out_grad, w_gate, w_up, w_down,
-    d_in, g_gate, g_up, g_down,
-    xin, wcat, og, wdn, pbuf, pr, s2, xr, yr, zg, zgr, zb, zbr, yb, dcat, hid, dzs, dzr, dxo, dxf, dxs, dxr, gs, gacc,
+    d_out, g_gate, g_up, g_out,
+    xin, wcat, og, wdn, pbuf, pr, s2, xr, yr, zg, zgr, zb, zbr, yb, dcat, hid, dzs, dzr, dxo, dxf, dxs, dxr, gs, gacc, d_in, g_down,
     ssem, rsem, lsem,
 ):
     i = lax.axis_index("in")
@@ -482,6 +482,7 @@
         else:
             recv(("dz", k), dzr.at[k, 0:64])
             d_in[at, :] = (dxf[DY.index(k), l, 0] + dzr[k, 0:64].astype(F32)).astype(BF16)
+        move(d_in.at[at, :], d_out.at[at, :])
 
     def grad_part(k, n, cols):
         at = pl.ds(al(n * 256, 256), 256)
@@ -533,6 +534,8 @@
                 hid[:, pl.ds(al(m * 256, 256), 256)], og[...].reshape(2048, 384), (((0,), (0,)), ((), ())),
                 preferred_element_type=F32,
             ).astype(BF16)
+
+        move(g_down, g_out)
 
     steps = (
         (stz, 1), (st_og, -1), (st_w, 0), (st_og, 0), (sty, 1), (fw, 1), (stz, 2), (ox, 3), (st_og, 1), (stz, 3),
@@ -579,7 +582,6 @@
 def shards(inputs, out_grad, w_gate, w_up, w_down):
     v = pltpu.VMEM
     any_ = pl.BlockSpec(memory_space=pl.ANY)
-    vm = pl.BlockSpec(memory_space=pltpu.VMEM)
     outs = pl.pallas_call(
         kernel,
         name="swiglu_back",
@@ -590,7 +592,7 @@
             jax.ShapeDtypeStruct((1024, 384), BF16),
         ),
         in_specs=[any_] * 5,
-        out_specs=(vm, any_, any_, vm),
+        out_specs=(any_,) * 4,
         scratch_shapes=[
             v((2048, 768), BF16),
             v((768, 1024), BF16),
@@ -616,6 +618,8 @@
             v((4, 3, 2, 64, 768), BF16),
             v((4, 768, 256), BF16),
             v((768, 1024), F32),
+            v((256, 768), BF16),
+            v((1024, 384), BF16),
             pltpu.SemaphoreType.DMA((N_SEM,)),
             pltpu.SemaphoreType.DMA((N_SEM,)),
             pltpu.SemaphoreType.DMA((20,)),

time: 120 us -> 119 us (level)
  no operation moved by 1% of the time
where the time goes in v6:
time: 119 us
  Pallas kernels  119 us (100%)
    pallas_call x1, Pallas kernels, shards(): pl.pallas_call(kernel, name='swiglu_back', out_shape=(jax.ShapeDtypeStruc...  116 us
    pallas_call x1, Pallas kernels, shards(): pl.pallas_call(finish, name='results', out_shape=tuple((jax.ShapeDtypeStr...  2.82 us

profile of v6, /device:TPU:1, one launch (start us, length us, event | category | flops | bytes accessed | tf_op | source)
XLA Modules:
  0.0 119.3 jit_solution(15675137633111276787)
XLA Ops:
  0.6 115.8 %swiglu_back.1 = (bf16[256,768]{1,0:T(8,128)(2,1)}, bf16[3072,128]{1,0:T(8,128)(2,1)}, bf16[3072,128]{1,0:T(8,128)(2,1)}, bf16[1024,384]{1,0:T(8,128)(2,1)}) custom-call(bf16[256,3072]{1,0:T(8,128)(2,1)} %inputs.1, bf16[4,4,16,3072]{3,2,1,0:T(8,128)(2,1)} %bitcast.1, bf16[3072,128]{1,0:T(8,128)(2,1)} %w_gate.1, bf16[3072,128]{1,0:T(8,128)(2,1)} %w_up.1, ...), custom_call_target="tpu_custom_call" | custom-call | flops 12999999488 | bytes 8388608 | tf_op jit(solution)/shard_map/swiglu_back/pallas_call | solution.py:585
  116.5 2.8 %results.1 = (bf16[256,768]{1,0:T(8,128)(2,1)}, bf16[3072,128]{1,0:T(8,128)(2,1)}, bf16[3072,128]{1,0:T(8,128)(2,1)}, bf16[1024,384]{1,0:T(8,128)(2,1)}) custom-call(bf16[256,768]{1,0:T(8,128)(2,1)} %get-tuple-element.8.refs_0_, bf16[3072,128]{1,0:T(8,128)(2,1)} %get-tuple-element.9.refs_1_, bf16[3072,128]{1,0:T(8,128)(2,1)} %get-tuple-element.10.refs_2_, ...), custom_call_target="tpu_custom_call" | custom-call | bytes 5242880 | tf_op jit(solution)/shard_map/results/pallas_call | solution.py:630
